TPU v7x, 32 devices: a whole 2x2x4 slice. The times are simulated.
32 devices in a mesh: seq: 2 (over y), fsdp: 16 (over z, x, core).
Axes of the slice: x: 2, y: 2, z: 4, core: 2. Of those that a mesh axis runs over, the one named last changes fastest.
Arguments:
- hidden: bfloat16 [16, 1024, 768], P('fsdp', 'seq'), may hold values from -6 to 6
- query_in: bfloat16 [16, 256, 768], P('fsdp', 'seq'), may hold values from -6 to 6
- memory: bfloat16 [16, 384, 768], P('fsdp', 'seq'), may hold values from -6 to 6
- segment_ids: int32 [16, 1408], P('fsdp'), may hold values from 0 to 2, never falling along the last dimension, each value on 1 to 704 neighbouring positions
- block_order: int32 [16, 4], P('fsdp'), may hold values from 0 to 3, each once within a row
- memory_valid: int32 [16, 384], P('fsdp'), may hold values 0 or 1
- w_query: bfloat16 [768, 768], P('fsdp'), may hold values from -0.21875 to 0.21875
- w_key: bfloat16 [768, 768], P('fsdp'), may hold values from -0.21875 to 0.21875
- w_value: bfloat16 [768, 768], P('fsdp'), may hold values from -0.21875 to 0.21875
- w_out: bfloat16 [768, 768], P('fsdp'), may hold values from -1.75 to 1.75
- w_rel: bfloat16 [768, 768], P('fsdp', 'seq'), may hold values from -0.21875 to 0.21875
- rel_biases: bfloat16 [3, 768], P(None, ('seq', 'fsdp')), may hold values from -3 to 3
- seg_embed: bfloat16 [2, 768], P(None, ('seq', 'fsdp')), may hold values from -3 to 3
- w_inner: bfloat16 [768, 3072], P('fsdp'), may hold values from -0.21875 to 0.21875
- b_inner: bfloat16 [3072], P('fsdp'), may hold values from -3 to 3
- w_outer: bfloat16 [3072, 768], P('fsdp'), may hold values from -0.109375 to 0.109375
- b_outer: bfloat16 [768], P('fsdp'), may hold values from -2 to 2
- norm_gains: bfloat16 [2, 768], P(None, 'fsdp'), may hold values from 0.5 to 1.5
- norm_biases: bfloat16 [2, 768], P(None, 'fsdp'), may hold values from -2 to 2
- grad_hidden_out: bfloat16 [16, 1024, 768], P('fsdp', 'seq'), may hold values from -6 to 6
- grad_query_out: bfloat16 [16, 256, 768], P('fsdp', 'seq'), may hold values from -6 to 6
Outputs:
- hidden_out: bfloat16 [16, 1024, 768], P('fsdp', 'seq')
- query_out: bfloat16 [16, 256, 768], P('fsdp', 'seq')
- grad_hidden: float32 [16, 1024, 768], P('fsdp', 'seq')
- grad_query: float32 [16, 256, 768], P('fsdp', 'seq')
- grad_w_query: float32 [768, 768], P(('seq', 'fsdp'))
- grad_w_key: float32 [768, 768], P(('seq', 'fsdp'))
- grad_w_value: float32 [768, 768], P(('seq', 'fsdp'))
- grad_w_out: float32 [768, 768], P(('seq', 'fsdp'))
- grad_w_rel: float32 [768, 768], P('fsdp', 'seq')
- grad_rel_biases: float32 [3, 768], P(None, ('seq', 'fsdp'))
- grad_seg_embed: float32 [2, 768], P(None, ('seq', 'fsdp'))
- grad_w_inner: float32 [768, 3072], P(('seq', 'fsdp'))
- grad_b_inner: float32 [3072], P(('seq', 'fsdp'))
- grad_w_outer: float32 [3072, 768], P(('seq', 'fsdp'))
- grad_b_outer: float32 [768], P(('seq', 'fsdp'))
- grad_norm_gains: float32 [2, 768], P(None, ('seq', 'fsdp'))
- grad_norm_biases: float32 [2, 768], P(None, ('seq', 'fsdp'))
Inputs may be any that keep to these rules, and one draw needn't show every extreme that they name: `segment_ids`: each row holds the segments of 384 memory slots, then of 1024 tokens, never falling. `block_order`: each row names each of the 4 blocks once.
All inputs are finite; a program needn't handle non-finite values. No bound on the sum of `memory_valid` on one device may be relied on, other than what follows from the above.
Results may differ from a plain program's by a relative error of at most 0.017.
Values may be sent and summed in bfloat16 or wider, within the bound.
No kernel may reach another device: no remote copies, remote signals or barrier semaphores. Data moves between devices by JAX's collectives and lax.ppermute only.
A program may use at most 256 MiB of HBM per device.

v0:
```python
import functools

import jax
import jax.numpy as jnp
from jax import lax
from jax.experimental import pallas as pl
from jax.experimental.pallas import tpu as pltpu
from jax.sharding import PartitionSpec as P

DH = 64
BLOCK = 256
NBLK = 4
MEM = 384
L = 1024
LANES = 128

QROW = L
MROW = L + BLOCK
ROWS = L + BLOCK + MEM
KEYS = MEM + L
SPAN_M = MEM + BLOCK
SPAN_T = 2 * BLOCK
REL_M = L - BLOCK
REL_T = MEM + L - BLOCK
REL_ROWS = MEM + 2 * L
SPANS = SPAN_M + NBLK * SPAN_T

EPSILON = 1e-05
NEGATIVE = -1e30
SCORE_SCALE = 0.125
EXP2_SCALE = SCORE_SCALE * 1.4426950408889634
STEPS = NBLK + 1
VMEM_LIMIT = 60 * 1024 * 1024
BF = jnp.bfloat16
F32 = jnp.float32


def product(left, right):
    return jnp.dot(left, right, preferred_element_type=F32)


def inner_rows(left, right):
    return lax.dot_general(left, right, (((1,), (1,)), ((), ())), preferred_element_type=F32)


def inner_cols(left, right):
    return lax.dot_general(left, right, (((0,), (0,)), ((), ())), preferred_element_type=F32)


def sinusoid(row_count, width_all, farthest):
    fine = DH
    frequency = 10000.0 ** (-jnp.arange(0, width_all, 2).astype(F32) / width_all)
    starts = (farthest - fine * jnp.arange(row_count // fine)).astype(F32)
    far = starts[:, None, None] * frequency
    near = jnp.arange(fine).astype(F32)[None, :, None] * frequency
    sines = jnp.sin(far) * jnp.cos(near) - jnp.cos(far) * jnp.sin(near)
    cosines = jnp.cos(far) * jnp.cos(near) + jnp.sin(far) * jnp.sin(near)
    return jnp.concatenate([sines, cosines], 2).reshape(row_count, width_all)


def split_low(values):
    high = values.astype(BF).astype(F32)
    return high, values - high


def place(step, order_ref):
    last = jnp.minimum(step, NBLK - 1)
    block = order_ref[last]
    row = jnp.where(step < NBLK, block, NBLK) * BLOCK
    return block, pl.multiple_of(row, BLOCK), last


def row_terms(q_ref, kx_ref, par_ref, row):
    query = q_ref[pl.ds(row, BLOCK), :].astype(F32)
    marks = kx_ref[pl.ds(row, BLOCK), :].astype(F32)
    return query + par_ref[0:1, :], query + par_ref[1:2, :], query + par_ref[2:3, :], marks


def gather_keys(order_ref, from_ref, to_ref, lanes):
    to_ref[:MEM, lanes] = from_ref[MROW:, :]
    for at in range(NBLK):
        rows = pl.ds(pl.multiple_of(BLOCK * order_ref[at], BLOCK), BLOCK)
        to_ref[MEM + BLOCK * at : MEM + BLOCK * (at + 1), lanes] = from_ref[rows, :]


def key_spots(order_ref, block, count):
    spots = [(0, MEM, pl.multiple_of(REL_M - BLOCK * block, BLOCK), 0)]
    for at in range(count):
        rel_row = pl.multiple_of(REL_T + BLOCK * (order_ref[at] - block), LANES)
        spots.append((MEM + BLOCK * at, BLOCK, rel_row, SPAN_M + SPAN_T * at))
    return spots


def gather_spans(spots, rel_ref, span_ref):
    for _, key_count, rel_row, put in spots:
        span = key_count + BLOCK
        span_ref[put : put + span, :] = rel_ref[pl.ds(rel_row, span), :]


def forward_kernel(
    order_ref,
    q_ref,
    k_ref,
    v_ref,
    rel_ref,
    kx_ref,
    par_ref,
    att_ref,
    exp_ref,
    inv_ref,
    kcat_ref,
    vcat_ref,
    score_ref,
    lhs_ref,
    qr_ref,
    span_ref,
    sum_ref,
):
    step = pl.program_id(0)

    @pl.when(step == 0)
    def _():
        gather_keys(order_ref, k_ref, kcat_ref, slice(0, LANES))
        gather_keys(order_ref, kx_ref, kcat_ref, slice(LANES, 2 * LANES))
        gather_keys(order_ref, v_ref, vcat_ref, slice(0, LANES))
        vcat_ref[:, LANES:] = jnp.ones((KEYS, LANES), BF)

    block, row, last = place(step, order_ref)
    lane = lax.broadcasted_iota(jnp.int32, (BLOCK, LANES), 1)
    query_w, query_r, query_s, marks = row_terms(q_ref, kx_ref, par_ref, row)
    same, other = query_s * par_ref[3:4, :], query_s * par_ref[4:5, :]
    for head in range(2):
        mine = (lane < DH) == (head == 0)
        other_sum = jnp.sum(jnp.where(mine, other, 0.0), -1, keepdims=True)
        diff = jnp.sum(jnp.where(mine, same, 0.0), -1, keepdims=True) - other_sum
        diff_high, diff_low = split_low(diff)
        other_high, other_low = split_low(other_sum)
        extra = jnp.where(lane < 3, marks * diff_high, jnp.where(lane < 6, marks * diff_low, 0.0))
        extra = jnp.where(lane == 6, other_high, jnp.where(lane == 7, other_low, extra))
        extra = jnp.where(lane == 8, NEGATIVE, extra)
        lhs_ref[head, :, :LANES] = jnp.where(mine, query_w, 0.0).astype(BF)
        lhs_ref[head, :, LANES:] = extra.astype(BF)
        qr_ref[head] = jnp.where(mine, query_r, 0.0).astype(BF)

    across = lax.broadcasted_iota(jnp.int32, (BLOCK, BLOCK), 0) - lax.broadcasted_iota(
        jnp.int32, (BLOCK, BLOCK), 1
    )
    hidden_at = jnp.where(step < NBLK, BLOCK, 0)

    for count in range(NBLK):

        @pl.when(last == count)
        def _():
            spots = key_spots(order_ref, block, count + 1)
            keys = MEM + BLOCK * (count + 1)
            spans = SPAN_M + SPAN_T * (count + 1)
            gather_spans(spots, rel_ref, span_ref)
            for head in range(2):
                content = inner_rows(lhs_ref[head], kcat_ref[:keys, :])
                position = inner_rows(qr_ref[head], span_ref[:spans, :])
                top = None
                for at, key_count, _, put in spots:
                    span = key_count + BLOCK
                    moved = position[:, put : put + span]
                    moved = pltpu.roll(moved, span - BLOCK + 1, 1, stride=1, stride_axis=0)
                    tile = content[:, at : at + key_count] + moved[:, :key_count]
                    if at + key_count == keys:
                        tile = jnp.where(across == hidden_at, NEGATIVE, tile)
                    score_ref[head, :, at : at + key_count] = tile
                    for piece in range(0, key_count, LANES):
                        part = tile[:, piece : piece + LANES]
                        top = part if top is None else jnp.maximum(top, part)
                peak = jnp.max(top, -1, keepdims=True)
                low = jnp.exp2((score_ref[head, :, :keys] - peak) * EXP2_SCALE).astype(BF)
                exp_ref[head, :, :keys] = low
                sum_ref[head] = product(low, vcat_ref[:keys, :])

    sums = sum_ref[0], sum_ref[1]
    first = lane < DH
    inverse = 1.0 / jnp.where(first, sums[0][:, LANES:], sums[1][:, LANES:])
    total = jnp.where(first, sums[0][:, :LANES], sums[1][:, :LANES])
    att_ref[pl.ds(row, BLOCK), :] = (total * inverse).astype(BF)
    inv_ref[pl.ds(row, BLOCK), :] = inverse


def backward_kernel(
    order_ref,
    q_ref,
    k_ref,
    v_ref,
    rel_ref,
    kx_ref,
    par_ref,
    grad_ref,
    att_ref,
    inv_ref,
    exp_ref,
    dqkv_ref,
    drel_ref,
    dpar_ref,
    kcat_ref,
    vcat_ref,
    flip_ref,
    lhs_ref,
    qwt_ref,
    qrt_ref,
    gt_ref,
    dkt_ref,
    dvt_ref,
    drelt_ref,
    accw_ref,
    accr_ref,
    span_ref,
    moved_ref,
):
    step = pl.program_id(0)

    @pl.when(step == 0)
    def _():
        gather_keys(order_ref, k_ref, kcat_ref, slice(0, LANES))
        gather_keys(order_ref, kx_ref, kcat_ref, slice(LANES, 2 * LANES))
        gather_keys(order_ref, v_ref, vcat_ref, slice(0, LANES))
        vcat_ref[:, :LANES] = (vcat_ref[:, :LANES].astype(F32) * SCORE_SCALE).astype(BF)
        vcat_ref[:, LANES:] = jnp.full((KEYS, LANES), SCORE_SCALE, BF)
        up = lax.broadcasted_iota(jnp.int32, (BLOCK, BLOCK), 0)
        down = lax.broadcasted_iota(jnp.int32, (BLOCK, BLOCK), 1)
        flip_ref[...] = jnp.where(up + down == BLOCK - 1, 1.0, 0.0).astype(BF)
        dkt_ref[...] = jnp.zeros_like(dkt_ref)
        dvt_ref[...] = jnp.zeros_like(dvt_ref)
        drelt_ref[...] = jnp.zeros_like(drelt_ref)
        dpar_ref[...] = jnp.zeros_like(dpar_ref)

    block, row, last = place(step, order_ref)
    lane = lax.broadcasted_iota(jnp.int32, (BLOCK, LANES), 1)
    first = lane < DH
    flip = flip_ref[...]
    rows = pl.ds(row, BLOCK)
    grad_low = (grad_ref[rows, :].astype(F32) * inv_ref[rows, :]).astype(BF)
    query, marks = product(flip, q_ref[rows, :]), product(flip, kx_ref[rows, :])
    grad, att = product(flip, grad_low), product(flip, att_ref[rows, :])
    query_w = query + par_ref[0:1, :]
    query_r = query + par_ref[1:2, :]
    query_s = query + par_ref[2:3, :]
    dots = grad * att
    for head in range(2):
        mine = first == (head == 0)
        high, low = split_low(-jnp.sum(jnp.where(mine, dots, 0.0), -1, keepdims=True))
        extra = jnp.where(lane == 0, high, jnp.where(lane == 1, low, 0.0))
        lhs_ref[head, :, :LANES] = jnp.where(mine, grad, 0.0).astype(BF)
        lhs_ref[head, :, LANES:] = extra.astype(BF)
    qwt_ref[...] = query_w.astype(BF).astype(F32).T.astype(BF)
    qrt_ref[...] = query_r.astype(BF).astype(F32).T.astype(BF)
    gt_ref[...] = grad_low.astype(F32).T.astype(BF)

    for count in range(NBLK):

        @pl.when(last == count)
        def _():
            spots = key_spots(order_ref, block, count + 1)
            keys = MEM + BLOCK * (count + 1)
            spans = SPAN_M + SPAN_T * (count + 1)
            gather_spans(spots, rel_ref, span_ref)
            for head in range(2):
                own = slice(DH * head, DH * head + DH)
                probs = exp_ref[head, :, :keys]
                slope = inner_rows(lhs_ref[head], vcat_ref[:keys, :])
                scaled = (product(flip, probs) * slope).astype(BF)
                for at, key_count, _, put in spots:
                    span = key_count + BLOCK
                    moved = jnp.concatenate(
                        [scaled[:, at : at + key_count], jnp.zeros((BLOCK, BLOCK), BF)], 1
                    )
                    moved_ref[head, :, put : put + span] = pltpu.roll(
                        moved, 0, 1, stride=1, stride_axis=0
                    )
                dkt_ref[own, :keys] += product(qwt_ref[own, :], scaled)
                dvt_ref[own, :keys] += product(gt_ref[own, :], probs)
                accw_ref[head] = product(scaled, kcat_ref[:keys, :])
                accr_ref[head] = product(moved_ref[head, :, :spans], span_ref[:spans, :])
                drel = product(qrt_ref[own, :], moved_ref[head, :, :spans])
                for _, key_count, rel_row, put in spots:
                    span = key_count + BLOCK
                    drelt_ref[own, pl.ds(rel_row, span)] += drel[:, put : put + span]

    grad_w = jnp.where(first, accw_ref[0, :, :LANES], accw_ref[1, :, :LANES])
    grad_r = jnp.where(first, accr_ref[0], accr_ref[1])
    same_sums, other_sums = [], []
    for head in range(2):
        sums = accw_ref[head, :, LANES:]
        same_sums.append(jnp.sum(jnp.where(lane < 3, marks * sums, 0.0), -1, keepdims=True))
        total = jnp.sum(jnp.where(lane == 6, sums, 0.0), -1, keepdims=True)
        other_sums.append(total - same_sums[head])
    same = jnp.where(first, same_sums[0], same_sums[1])
    other = jnp.where(first, other_sums[0], other_sums[1])
    grad_s = same * par_ref[3:4, :] + other * par_ref[4:5, :]
    high, low = split_low(grad_w + grad_r + grad_s)
    dqkv_ref[rows, :LANES] = (
        product(flip, high.astype(BF)) + product(flip, low.astype(BF))
    ).astype(BF)
    for at, terms in enumerate((grad_w, grad_r, grad_s, same * query_s, other * query_s)):
        dpar_ref[at : at + 1, :] += jnp.sum(terms, 0, keepdims=True)

    @pl.when(step == STEPS - 1)
    def _():
        dqkv_ref[MROW:, :LANES] = jnp.zeros((MEM, LANES), BF)
        dqkv_ref[L:MROW, LANES:] = jnp.zeros((BLOCK, 2 * LANES), BF)
        for lanes, from_ref in ((1, dkt_ref), (2, dvt_ref)):
            lanes = slice(lanes * LANES, (lanes + 1) * LANES)
            dqkv_ref[MROW:, lanes] = from_ref[:, :MEM].T.astype(BF)
            for at in range(NBLK):
                rows_at = pl.ds(pl.multiple_of(BLOCK * order_ref[at], BLOCK), BLOCK)
                start = MEM + BLOCK * at
                dqkv_ref[rows_at, lanes] = from_ref[:, start : start + BLOCK].T.astype(BF)
        drel_ref[...] = drelt_ref[...].T.astype(BF)


def column(rows, at):
    return pl.BlockSpec((rows, LANES), lambda step, order: (0, at))


def attention_specs(pair, first):
    ins = [column(ROWS, first + at) for at in range(3)]
    ins += [column(REL_ROWS, pair), column(ROWS, 0), column(8, pair)]
    exps = pl.BlockSpec((None, 2, BLOCK, KEYS), lambda step, order: (step, 0, 0, 0))
    return ins, exps


def settings(passes):
    return dict(
        compiler_params=pltpu.CompilerParams(
            dimension_semantics=("arbitrary",), vmem_limit_bytes=40 * 1024 * 1024
        ),
        cost_estimate=pl.CostEstimate(
            flops=passes * 4 * MROW * KEYS * BLOCK,
            bytes_accessed=STEPS * 2 * BLOCK * KEYS * 2,
            transcendentals=2 * MROW * KEYS,
        ),
    )


def attention_forward(pair, first, order, qkv, rel, marks, par):
    ins, exps = attention_specs(pair, first)
    return pl.pallas_call(
        forward_kernel,
        grid_spec=pltpu.PrefetchScalarGridSpec(
            num_scalar_prefetch=1,
            grid=(STEPS,),
            in_specs=ins,
            out_specs=[column(MROW, 0), exps, column(MROW, 0)],
            scratch_shapes=[
                pltpu.VMEM((KEYS, 2 * LANES), BF),
                pltpu.VMEM((KEYS, 2 * LANES), BF),
                pltpu.VMEM((2, BLOCK, KEYS), F32),
                pltpu.VMEM((2, BLOCK, 2 * LANES), BF),
                pltpu.VMEM((2, BLOCK, LANES), BF),
                pltpu.VMEM((SPANS, LANES), BF),
                pltpu.VMEM((2, BLOCK, 2 * LANES), F32),
            ],
        ),
        out_shape=[
            jax.ShapeDtypeStruct((MROW, LANES), BF),
            pltpu.HBM((STEPS, 2, BLOCK, KEYS), BF),
            jax.ShapeDtypeStruct((MROW, LANES), F32),
        ],
        **settings(16),
    )(order, qkv, qkv, qkv, rel, marks, par)


def attention_backward(pair, first, order, qkv, rel, marks, par, grad, att, inverse, exps_in):
    ins, exps = attention_specs(pair, first)
    qkv, rel, exps_in = (
        pltpu.with_memory_space_constraint(t, pltpu.HBM) for t in (qkv, rel, exps_in)
    )
    return pl.pallas_call(
        backward_kernel,
        grid_spec=pltpu.PrefetchScalarGridSpec(
            num_scalar_prefetch=1,
            grid=(STEPS,),
            in_specs=ins + [column(MROW, 0)] * 3 + [exps],
            out_specs=[
                pl.BlockSpec((ROWS, 3 * LANES), lambda step, order: (0, 0)),
                column(REL_ROWS, 0),
                column(8, 0),
            ],
            scratch_shapes=[
                pltpu.VMEM((KEYS, 2 * LANES), BF),
                pltpu.VMEM((KEYS, 2 * LANES), BF),
                pltpu.VMEM((BLOCK, BLOCK), BF),
                pltpu.VMEM((2, BLOCK, 2 * LANES), BF),
                pltpu.VMEM((LANES, BLOCK), BF),
                pltpu.VMEM((LANES, BLOCK), BF),
                pltpu.VMEM((LANES, BLOCK), BF),
                pltpu.VMEM((LANES, KEYS), F32),
                pltpu.VMEM((LANES, KEYS), F32),
                pltpu.VMEM((LANES, REL_ROWS), F32),
                pltpu.VMEM((2, BLOCK, 2 * LANES), F32),
                pltpu.VMEM((2, BLOCK, LANES), F32),
                pltpu.VMEM((SPANS, LANES), BF),
                pltpu.VMEM((2, BLOCK, SPANS), BF),
            ],
        ),
        out_shape=[
            jax.ShapeDtypeStruct((ROWS, 3 * LANES), BF),
            jax.ShapeDtypeStruct((REL_ROWS, LANES), BF),
            jax.ShapeDtypeStruct((8, LANES), F32),
        ],
        **settings(24),
    )(order, qkv, qkv, qkv, rel, marks, par, grad, att, inverse, exps_in)


CHUNKS = 2


def norm_parts(values):
    center = values - jnp.mean(values, -1, keepdims=True)
    spread = jnp.mean(center * center, -1, keepdims=True)
    scale = lax.rsqrt(spread + EPSILON)
    return center * scale, scale


def norm_pull(grad, unit, scale, gain):
    grad = grad * gain
    mean = jnp.mean(grad, -1, keepdims=True)
    slope = jnp.mean(grad * unit, -1, keepdims=True)
    return (grad - mean - unit * slope) * scale


def dealt(values, groups):
    if groups is None:
        return values.astype(BF)
    share = values.shape[0] // (2 * groups)
    pieces = [
        values[(side * groups + at) * share :][:share] for at in range(groups) for side in range(2)
    ]
    return jnp.concatenate(pieces, 0).astype(BF)


def middle_kernel(
    groups,
    side_ref,
    attn_ref,
    hidden_ref,
    query_ref,
    grad_hidden_ref,
    grad_query_ref,
    weights_ref,
    inner_bias_ref,
    small_ref,
    result_ref,
    grad_sum_ref,
    grad_attn_ref,
    gw_ref,
    gb_inner_ref,
    g_small_ref,
    unit_ref,
    scale_ref,
    low_ref,
    low_t_ref,
    act_ref,
    slope_ref,
    sum_ref,
    grad_ref,
    grad_low_ref,
    back_ref,
    held_ref,
    arrived,
):
    step = pl.program_id(0)
    rows, width = attn_ref.shape
    tiles = act_ref.shape[1] // width
    half = hidden_ref.shape[0]
    cut = rows // CHUNKS
    gain_one, shift_one = small_ref[0:1, :], small_ref[1:2, :]
    gain_two, shift_two = small_ref[2:3, :], small_ref[3:4, :]
    parts = [slice(at * cut, at * cut + cut) for at in range(CHUNKS)]

    def fetch(at):
        columns = pl.ds(pl.multiple_of(at * width, width), width)
        return pltpu.make_async_copy(weights_ref.at[:, columns], held_ref.at[at], arrived.at[at])

    @pl.when(step == 0)
    def _():
        fetch(0).start()
        for at in range(tiles):
            fetch(1 + at).start()
            fetch(1 + tiles + at).start()
        fetch(0).wait()
        sum_ref[...] = product(attn_ref[...], held_ref[0])
        sum_ref[:half, :] += hidden_ref[...].astype(F32)
        sum_ref[half:, :] += query_ref[...].astype(F32)
        for part in parts:
            unit, scale = norm_parts(sum_ref[part, :])
            unit_ref[part, :] = unit
            scale_ref[part, :] = jnp.broadcast_to(scale, (cut, LANES))
            first = unit * gain_one + shift_one
            low_ref[part, :] = first.astype(BF)
            sum_ref[part, :] = first + small_ref[4:5, :]

    place_of = jnp.where(step < tiles, step, jnp.minimum(lax.div(step - tiles, 2), tiles - 1))
    columns = pl.ds(pl.multiple_of(place_of * width, width), width)

    w_inner, w_outer = held_ref.at[1 + place_of], held_ref.at[1 + tiles + place_of]

    @pl.when(step < tiles)
    def _():
        fetch(1 + step).wait()
        fetch(1 + tiles + step).wait()
        for part in parts:
            pre = product(low_ref[part, :], w_inner[...]) + inner_bias_ref[...]
            square = pre * pre
            bend = jnp.tanh(0.7978845608028654 * (pre + 0.044715 * square * pre))
            half_bend = 0.5 + 0.5 * bend
            wide = pre * half_bend
            act = wide.astype(BF)
            act_ref[part, columns] = act
            turn = 1.5957691216057308 + 0.2140644488 * square
            slope_ref[part, columns] = half_bend + wide * (1.0 - half_bend) * turn
            sum_ref[part, :] += product(act, w_outer[...])

    @pl.when(step == tiles - 1)
    def _():
        g_gain = g_shift = g_outer = 0.0
        grad_ref[:half, :] = grad_hidden_ref[...].astype(F32)
        grad_ref[half:, :] = grad_query_ref[...].astype(F32)
        for part in parts:
            unit, scale = norm_parts(sum_ref[part, :])
            result_ref[part, :] = (unit * gain_two + shift_two).astype(BF)
            grad = grad_ref[part, :]
            g_gain += jnp.sum(grad * unit, 0, keepdims=True)
            g_shift += jnp.sum(grad, 0, keepdims=True)
            grad = norm_pull(grad, unit, scale, gain_two)
            low = grad.astype(BF)
            grad_ref[part, :] = grad
            grad_low_ref[part, :] = low
            g_outer += jnp.sum(low.astype(F32), 0, keepdims=True)
        g_small_ref[...] = jnp.zeros_like(g_small_ref)
        g_small_ref[2:3, :] = g_gain
        g_small_ref[3:4, :] = g_shift
        g_small_ref[4:5, :] = g_outer
        low_t_ref[...] = low_ref[...].T

    turn_back = jnp.logical_and(step >= tiles, step < 3 * tiles)

    @pl.when(jnp.logical_and(turn_back, lax.rem(step - tiles, 2) == 0))
    def _():
        g_inner = 0.0
        for part in parts:
            back = inner_rows(grad_low_ref[part, :], w_outer[...])
            low = (back * slope_ref[part, columns]).astype(BF)
            back_ref[part, :] = low
            g_inner += jnp.sum(low.astype(F32), 0, keepdims=True)
            grad_ref[part, :] += inner_rows(low, w_inner[...])
        gb_inner_ref[...] = g_inner
        gw_ref[...] = dealt(product(low_t_ref[...], back_ref[...]), groups)

    @pl.when(jnp.logical_and(turn_back, lax.rem(step - tiles, 2) == 1))
    def _():
        gw_ref[...] = dealt(inner_cols(act_ref[:, columns], grad_low_ref[...]), groups)

    @pl.when(step == 3 * tiles)
    def _():
        g_gain = g_shift = 0.0
        for part in parts:
            unit, scale = unit_ref[part, :], scale_ref[part, 0:1]
            grad = grad_ref[part, :]
            g_gain += jnp.sum(grad * unit, 0, keepdims=True)
            g_shift += jnp.sum(grad, 0, keepdims=True)
            grad = norm_pull(grad, unit, scale, gain_one)
            grad_sum_ref[part, :] = grad
            grad_low_ref[part, :] = grad.astype(BF)
        g_small_ref[0:1, :] = g_gain
        g_small_ref[1:2, :] = g_shift
        gw_ref[...] = dealt(inner_cols(attn_ref[...], grad_low_ref[...]), groups)
        back = inner_rows(grad_low_ref[...], held_ref[0]).astype(BF)
        left = side_ref[0] == 0
        middle_at = width // 2
        for at in range(0, middle_at, LANES):
            near, far = back[:, at : at + LANES], back[:, middle_at + at :][:, :LANES]
            grad_attn_ref[0, at // LANES] = jnp.where(left, near, far)
            grad_attn_ref[1, at // LANES] = jnp.where(left, far, near)


def middle(groups, side, attn, hidden, query, grad_hidden, grad_query, weights, inner_bias, small):
    rows, width = attn.shape
    tiles = inner_bias.shape[1] // width

    def whole(array):
        return pl.BlockSpec(array.shape, lambda step, side: (0,) * array.ndim)

    def square(at):
        return pl.BlockSpec((width, width), lambda step, side: (0, at(step)))

    def back(step):
        return lax.min(lax.div(lax.max(step - tiles, 0), 2), tiles - 1)

    def tile(step):
        return lax.select(step < tiles, step, back(step))

    def written(step):
        odd = lax.rem(lax.max(step - tiles, 0), 2)
        return lax.select(step == 3 * tiles, 0, 1 + back(step) + tiles * odd)

    outs = [
        jax.ShapeDtypeStruct((rows, width), BF),
        jax.ShapeDtypeStruct((rows, width), F32),
        jax.ShapeDtypeStruct((2, width // 2 // LANES, rows, LANES), BF),
        jax.ShapeDtypeStruct((width, (1 + 2 * tiles) * width), BF),
        jax.ShapeDtypeStruct((1, tiles * width), F32),
        jax.ShapeDtypeStruct((8, width), F32),
    ]
    return pl.pallas_call(
        functools.partial(middle_kernel, groups),
        grid_spec=pltpu.PrefetchScalarGridSpec(
            num_scalar_prefetch=1,
            grid=(1 + 3 * tiles,),
            in_specs=[whole(t) for t in (attn, hidden, query, grad_hidden, grad_query)]
            + [
                pl.BlockSpec(memory_space=pl.ANY),
                pl.BlockSpec((1, width), lambda step, side: (0, tile(step))),
                whole(small),
            ],
            out_specs=[whole(t) for t in outs[:3]]
            + [
                square(written),
                pl.BlockSpec((1, width), lambda step, side: (0, back(step))),
                whole(outs[5]),
            ],
            scratch_shapes=[
                pltpu.VMEM((rows, width), F32),
                pltpu.VMEM((rows, LANES), F32),
                pltpu.VMEM((rows, width), BF),
                pltpu.VMEM((width, rows), BF),
                pltpu.VMEM((rows, tiles * width), BF),
                pltpu.VMEM((rows, tiles * width), F32),
                pltpu.VMEM((rows, width), F32),
                pltpu.VMEM((rows, width), F32),
                pltpu.VMEM((rows, width), BF),
                pltpu.VMEM((rows, width), BF),
                pltpu.VMEM((1 + 2 * tiles, width, width), BF),
                pltpu.SemaphoreType.DMA((1 + 2 * tiles,)),
            ],
        ),
        out_shape=outs,
        compiler_params=pltpu.CompilerParams(
            dimension_semantics=("arbitrary",), vmem_limit_bytes=VMEM_LIMIT
        ),
        cost_estimate=pl.CostEstimate(
            flops=12 * rows * width * width * tiles,
            bytes_accessed=20 * width * width * tiles,
            transcendentals=rows * width * tiles,
        ),
    )(side, attn, hidden, query, grad_hidden, grad_query, weights, inner_bias, small)


def swap(values):
    return lax.ppermute(values, "seq", [(0, 1), (1, 0)])


def bit_orders(groups):
    high = list(range(groups.bit_length() - 2, 0, -1))
    return high, high[-1:] + high[:-1]


def across(values, groups, bit):
    return lax.ppermute(values, "fsdp", [(i, i ^ (1 << bit)) for i in range(groups)])


def merged(values, theirs, place, held, bit):
    axis = sum(1 for other in held if other > bit)
    return jnp.where(
        (place >> bit) & 1 == 0,
        jnp.stack([values, theirs], axis),
        jnp.stack([theirs, values], axis),
    )


def gather_beside(one, two, groups, chunks, beside):
    place = lax.axis_index("fsdp")
    order_one, order_two = bit_orders(groups)
    order_one, order_two = order_one + [0], order_two + [0]
    swapped, late = [], []
    for at, (bit_one, bit_two) in enumerate(zip(order_one, order_two)):
        left = len(order_one) - at
        take = chunks[: -(-len(chunks) // left)] if len(chunks) >= left else []
        chunks = chunks[len(take) :]
        theirs = [across(one, groups, bit_one), across(two, groups, bit_two)]
        theirs += [swap(chunk) for chunk in take]
        if at == 1:
            theirs, beside = lax.optimization_barrier((theirs, beside))
        else:
            theirs = lax.optimization_barrier(theirs)
        if at == len(order_one) - 2:
            late = theirs[:2]
        one = merged(one, theirs[0], place, order_one[:at], bit_one)
        two = merged(two, theirs[1], place, order_two[:at], bit_two)
        swapped += theirs[2:]
    bits = len(order_one)
    return (
        one.reshape((-1,) + one.shape[bits + 1 :]),
        two.reshape((-1,) + two.shape[bits + 1 :]),
        swapped,
        beside,
        late,
    )


def shuffle(count, lanes):
    take = jnp.arange(count * lanes)[:, None]
    give = jnp.arange(count * lanes)[None, :]
    return ((take % lanes) * count + take // lanes == give).astype(BF)


def pad_to(values, count):
    return jnp.pad(values, (0, count - values.shape[0]))


def shards(
    hidden,
    query_in,
    memory,
    segment_ids,
    block_order,
    memory_valid,
    w_query,
    w_key,
    w_value,
    w_out,
    w_rel,
    rel_biases,
    seg_embed,
    w_inner,
    b_inner,
    w_outer,
    b_outer,
    norm_gains,
    norm_biases,
    grad_hidden_out,
    grad_query_out,
):
    side = lax.axis_index("seq")
    groups = lax.axis_size("fsdp")
    place_at = lax.axis_index("fsdp")
    half, width = hidden.shape[1:]
    target_half = query_in.shape[1]
    memory_half = memory.shape[1]
    head_width = w_rel.shape[1]
    shard_rows = w_query.shape[0]
    ffn_width = w_inner.shape[1]
    own_rows = half + target_half

    def by_side(own, other, axis):
        return jnp.where(
            side == 0,
            jnp.concatenate([own, other], axis),
            jnp.concatenate([other, own], axis),
        )

    pairs = head_width // LANES
    pair_width = 3 * LANES

    def head_columns(weight, pair):
        return lax.dynamic_slice_in_dim(weight, side * head_width + pair * LANES, LANES, 1)

    def pair_columns(pair):
        return [head_columns(weight, pair) for weight in (w_query, w_key, w_value)]

    order = block_order[0]
    segs = segment_ids[0]
    target_seg = lax.dynamic_slice_in_dim(segs, MEM + order[NBLK - 1] * BLOCK, BLOCK)
    seg_rows = jnp.concatenate([segs[MEM:], target_seg, segs[:MEM]])
    invalid = jnp.concatenate([jnp.zeros((MROW,), jnp.int32), (memory_valid[0] != 1).astype(jnp.int32)])
    lane = jnp.arange(LANES)[None, :]
    marks = jnp.where(lane < 6, seg_rows[:, None] == lane % 3, (lane == 6) | (lane == 7))
    marks = jnp.where(lane == 8, invalid[:, None] == 1, marks).astype(BF)

    pos_table = sinusoid(REL_ROWS, width, MEM + L - 1).astype(BF)
    few = jnp.concatenate([rel_biases, seg_embed], 0)
    few = jnp.pad(few, ((0, shard_rows - 5), (0, LANES - few.shape[1])))
    quarter = half // 2
    weights_one, weights_two, swapped, (pos_table, marks), late = gather_beside(
        jnp.concatenate(sum([pair_columns(pair) for pair in range(pairs - 1)], []), 1),
        jnp.concatenate(pair_columns(pairs - 1) + [w_rel, few], 1),
        groups,
        [hidden[0, :quarter], hidden[0, quarter:], memory[0], query_in[0]],
        (pos_table, marks),
    )
    rel_weight = weights_two[:, pair_width : pair_width + head_width]
    few_all = weights_two[:, pair_width + head_width :].reshape(groups, shard_rows, LANES)
    few_all = few_all[:, :5, : head_width // groups].astype(F32)
    few_all = few_all.transpose(1, 0, 2).reshape(5, head_width)

    blocks = ffn_width // width
    spots = shuffle(blocks, LANES)
    smalls = (b_inner, b_outer, norm_gains, norm_biases)
    small_flat = pad_to(jnp.concatenate([t.reshape(-1) for t in smalls]), shard_rows * LANES)
    inner_moved = lax.dot_general(
        w_inner.reshape(shard_rows, -1, blocks * LANES),
        spots,
        (((2,), (1,)), ((), ())),
        preferred_element_type=F32,
    ).astype(BF)
    inner_moved = inner_moved.reshape(shard_rows, -1, blocks, LANES).transpose(0, 2, 1, 3)
    mixed = jnp.concatenate(
        [
            w_out,
            inner_moved.reshape(shard_rows, ffn_width),
            w_outer.reshape(shard_rows, ffn_width),
            small_flat.reshape(shard_rows, LANES),
        ],
        1,
    )
    mixed, _ = lax.optimization_barrier((mixed, late))
    mixed = lax.all_gather(mixed, "fsdp", axis=0, tiled=True)
    small_all = mixed[:, width + 2 * ffn_width :].reshape(groups, shard_rows * LANES).astype(F32)

    def unpack():
        found, at = [], 0
        for small in smalls:
            piece = small_all[:, at : at + small.size].reshape((groups,) + small.shape)
            found.append(jnp.moveaxis(piece, 0, -2).reshape(small.shape[:-1] + (-1,)))
            at += small.size
        return found

    inner_bias, outer_bias, gains, shifts = unpack()

    cuts = ((0, half), (half, own_rows))
    far_hidden = jnp.concatenate(swapped[:2], 0)
    stacked = jnp.concatenate(
        [
            by_side(hidden[0], far_hidden, 0),
            by_side(query_in[0], swapped[3], 0),
            by_side(memory[0], swapped[2], 0),
        ],
        0,
    )

    qkv_one = product(stacked, weights_one).astype(BF)
    qkv_two = product(stacked, weights_two[:, :pair_width]).astype(BF)
    rel = product(pos_table, rel_weight).astype(BF)
    par = jnp.concatenate([few_all, jnp.zeros((3, head_width), F32)], 0)
    def rows_of(values, which):
        return jnp.concatenate(
            [
                lax.dynamic_slice_in_dim(values, which * half, half, 0),
                lax.dynamic_slice_in_dim(values, L + which * target_half, target_half, 0),
            ],
            0,
        )

    def pair_args(pair):
        last = pair == pairs - 1
        at = (0, qkv_two) if last else (3 * pair, qkv_one)
        return (pair, at[0], order, at[1], rel, marks, par)

    kept = []
    own_att, far_att = [], []
    for pair in range(pairs):
        att, exps, inverse = attention_forward(*pair_args(pair))
        kept.append((att, inverse, exps))
        own_att.append(rows_of(att, side))
        far_att.append(swap(rows_of(att, 1 - side)))
    attn_rows = by_side(jnp.concatenate(own_att, 1), jnp.concatenate(far_att, 1), 1)
    small = jnp.stack([gains[0], shifts[0], gains[1], shifts[1], outer_bias] + [outer_bias] * 3)
    devices = 2 * groups
    out_rows = width // devices
    dealt_rows = out_rows % 8 == 0
    result, grad_sum_one, grad_attn, grad_weights, grad_b_inner, grad_small = middle(
        groups if dealt_rows else None,
        side.astype(jnp.int32)[None],
        attn_rows,
        hidden[0],
        query_in[0],
        grad_hidden_out[0],
        grad_query_out[0],
        mixed,
        inner_bias.reshape(width, blocks).T.reshape(1, ffn_width),
        small,
    )

    if dealt_rows:
        token_sums = lax.psum_scatter(grad_weights, "fsdp", scatter_dimension=0, tiled=True)
        token_sums = token_sums.reshape(2, out_rows, -1)
        near_sums = lax.dynamic_index_in_dim(token_sums, side, 0, True)
        far_sums = swap(lax.dynamic_index_in_dim(token_sums, 1 - side, 0, True))
        token_sums = jnp.concatenate([near_sums, far_sums], 0)
    else:
        token_sums = lax.psum_scatter(
            grad_weights, ("seq", "fsdp"), scatter_dimension=0, tiled=True
        )[None]
    grad_b_inner = grad_b_inner.reshape(blocks, width).T.reshape(devices, -1)
    row_count = width // devices
    token_flat = jnp.concatenate(
        [
            grad_b_inner.reshape(devices, -1),
            grad_small[:5].reshape(5, devices, -1).transpose(1, 0, 2).reshape(devices, -1),
        ],
        1,
    )
    inner_count = ffn_width // devices

    weights_two = weights_two[:, :pair_width]
    weights_one, weights_two, attn_rows = lax.optimization_barrier(
        (weights_one, weights_two, attn_rows)
    )
    far_one, far_two = swap(weights_one), swap(weights_two)

    far_grads = [swap(grad_attn[1, pair]) for pair in range(pairs)]

    core = place_at % 2
    same_core = [[at for at in range(groups) if at % 2 == which] for which in range(2)]

    def core_pieces(parts, which):
        parts = [part.reshape((groups // 2, 2) + part.shape[1:]) for part in parts]
        parts = [lax.dynamic_index_in_dim(part, which, 1, False) for part in parts]
        message = jnp.concatenate(parts[:2], 2)
        return jnp.concatenate([message] + parts[2:], 1) if parts[2:] else message

    def core_message(parts):
        far = across(core_pieces(parts, 1 - core), groups, 0)
        near = core_pieces(parts, core)
        return (near.astype(F32) + far.astype(F32)).astype(BF)

    def sum_message(message):
        message = lax.all_to_all(
            message,
            "fsdp",
            split_axis=0,
            concat_axis=0,
            tiled=True,
            axis_index_groups=same_core,
        )
        return jnp.sum(message.astype(F32), 0)

    own_rows_grads, far_rows_grads, sums, few_grads = [], [], [], []
    for pair in range(pairs):
        own, far = grad_attn[0, pair], far_grads[pair]
        if pair:
            own, message, sums = lax.optimization_barrier((own, message, sums))
            sums.append(sum_message(message))
        head_grad = jnp.concatenate([by_side(own[a:b], far[a:b], 0) for a, b in cuts], 0)
        dqkv, drel, dpar = attention_backward(*pair_args(pair), head_grad, *kept[pair])
        if pair:
            dqkv, drel, sums = lax.optimization_barrier((dqkv, drel, sums))
        few_grads.append(dpar[:5])
        own_rows_grads.append(rows_of(dqkv, side))
        far_rows_grads.append(swap(rows_of(dqkv, 1 - side)))
        grad_pair = inner_cols(stacked, dqkv).astype(BF)
        grad_pair = grad_pair.reshape(2, groups, out_rows, pair_width).transpose(1, 0, 2, 3)
        parts = [
            grad_pair.reshape(groups, shard_rows, pair_width),
            inner_cols(pos_table, drel).astype(BF).reshape(groups, shard_rows, LANES),
        ]
        if pair == 0:
            token_flat = token_flat.reshape(2, groups, -1).transpose(1, 0, 2).astype(BF)
            extra = ((0, 0), (0, 6), (0, pair_width + LANES - token_flat.shape[2]))
            parts.append(jnp.pad(token_flat, extra))
        if pair == pairs - 1:
            few = jnp.concatenate(few_grads, 1).reshape(5, groups, head_width // groups)
            few = few.transpose(1, 0, 2).reshape(groups, 1, -1).astype(BF)
            few = jnp.pad(few, ((0, 0), (0, 7), (0, pair_width + LANES - few.shape[2])))
            parts.append(few)
        message = core_message(parts)
    sums.append(sum_message(message))
    sums, token_sums = lax.optimization_barrier((sums, token_sums))
    shares = token_sums.shape[0]
    plain = jnp.sum(token_sums.astype(F32), 0)
    out_out = plain[:, :width]
    out_outer = plain[:, width + ffn_width :].reshape(blocks * out_rows, width)
    inner_sums = token_sums[:, :, width : width + ffn_width]
    inner_sums = inner_sums.reshape(shares, out_rows, blocks, -1, LANES).transpose(1, 3, 0, 2, 4)
    out_inner = product(
        inner_sums.reshape(out_rows, -1, shares * blocks * LANES),
        jnp.concatenate([spots] * shares, 0),
    ).reshape(out_rows, ffn_width)

    early = slice(0, pairs - 1)
    grad_own = grad_sum_one + inner_rows(
        jnp.concatenate(own_rows_grads + far_rows_grads[early], 1),
        jnp.concatenate([weights_one, weights_two, far_one], 1),
    )
    grad_own = grad_own + inner_rows(far_rows_grads[-1], far_two)

    both_sums = jnp.concatenate([t[:shard_rows, :pair_width] for t in sums], 1)
    own_sum = lax.dynamic_slice_in_dim(both_sums, side * out_rows, out_rows, 0)
    far_sum = lax.dynamic_slice_in_dim(both_sums, (1 - side) * out_rows, out_rows, 0)
    far_sum = swap(far_sum.astype(BF)).astype(F32)
    small_sums = lax.dynamic_index_in_dim(sums[0], shard_rows + side, 0, False)
    small_sums += swap(
        lax.dynamic_index_in_dim(sums[0], shard_rows + 1 - side, 0, False).astype(BF)
    ).astype(F32)
    out_b_inner = small_sums[:inner_count]
    out_rest = small_sums[inner_count : inner_count + 5 * row_count].reshape(5, row_count)
    out_gains, out_shifts, out_b_outer = out_rest[0:4:2], out_rest[1:4:2], out_rest[4]

    def weight_rows(values, which):
        return [
            values[:, pair * pair_width + which * LANES :][:, :LANES] for pair in range(pairs)
        ]

    out_query, out_key, out_value = (
        by_side(
            jnp.concatenate(weight_rows(own_sum, which), 1),
            jnp.concatenate(weight_rows(far_sum, which), 1),
            1,
        )
        for which in range(3)
    )
    out_rel = jnp.concatenate([t[:shard_rows, pair_width:] for t in sums], 1)
    few_sum = sums[-1][shard_rows, : 5 * (head_width // groups)].reshape(5, -1)
    out_biases, out_seg = few_sum[:3], few_sum[3:]
    return (
        result[None, :half],
        result[None, half:],
        grad_own[None, :half],
        grad_own[None, half:],
        out_query,
        out_key,
        out_value,
        out_out,
        out_rel,
        out_biases,
        out_seg,
        out_inner,
        out_b_inner,
        out_outer,
        out_b_outer,
        out_gains,
        out_shifts,
    )


def solution(mesh):
    rows = P("fsdp", "seq", None)
    both = ("seq", "fsdp")
    in_specs = (
        (rows,) * 3
        + (P("fsdp", None),) * 7
        + (P("fsdp", "seq"), P(None, both), P(None, both))
        + (P("fsdp", None), P("fsdp"), P("fsdp", None), P("fsdp"))
        + (P(None, "fsdp"), P(None, "fsdp"))
        + (rows,) * 2
    )
    out_specs = (
        (rows,) * 4
        + (P(both, None),) * 4
        + (P("fsdp", "seq"), P(None, both), P(None, both))
        + (P(both, None), P(both), P(both, None), P(both))
        + (P(None, both), P(None, both))
    )
    return jax.shard_map(shards, mesh=mesh, in_specs=in_specs, out_specs=out_specs, check_vma=False)
```

profile of v0, /device:TPU:30, one launch (start us, length us, event | category | flops | bytes accessed | tf_op | source)
XLA Modules:
  0.0 360.8 jit_solution(4141504493304513641)
XLA Ops:
  14.1 1.2 slice_bitcast_fusion.3
  15.8 1.5 collective-permute-start.5
  19.3 1.2 slice.307
  22.6 1.5 fusion.7
  24.9 1.1 reshape.1022
  26.2 1.2 subtract_convert_fusion
  27.4 1.2 select_convert_fusion.kx_ref
  28.6 2.2 pad_maximum_fusion
  31.0 2.7 collective-permute-start.4
  34.3 1.6 collective-permute-done.5
  35.9 5.4 %collective-permute-done.3 = bf16[2,48,768]{2,1,0:T(8,128)(2,1)S(1)} collective-permute-done((bf16[2,48,768]{2,1,0:T(8,128)(2,1)S(1)}, bf16[2,48,768]{2,1,0:T(8,128)(2,1)S(1)}, u32[]{:S(2)}, u32[]{:S(2)}) %collective-permute-start.3) | collective-permute-done | bytes 147488 | tf_op jit(solution)/shard_map/ppermute | solution.py:665
  42.5 1.5 collective-permute-start.6
  44.9 4.8 %collective-permute-done.6 = bf16[2,2,48,768]{3,2,1,0:T(8,128)(2,1)S(1)} collective-permute-done((bf16[2,2,48,768]{3,2,1,0:T(8,128)(2,1)}, bf16[2,2,48,768]{3,2,1,0:T(8,128)(2,1)S(1)}, u32[]{:S(2)}, u32[]{:S(2)}) %collective-permute-start.6) | collective-permute-done | bytes 294944 | tf_op jit(solution)/shard_map/ppermute | solution.py:665
  50.4 1.5 collective-permute-start.11
  53.1 2.9 maximum_select_fusion
  58.1 2.2 maximum_select_fusion.5
  61.5 1.1 maximum_select_fusion.6
  62.7 2.6 maximum_select_fusion.2
  65.3 4.3 %convolution_convert_fusion.rel_ref = bf16[2432,384]{1,0:T(8,128)(2,1)S(1)} fusion(bf16[2432,768]{1,0:T(8,128)(2,1)} %pad_maximum_fusion, bf16[768,896]{1,0:T(8,128)(2,1)S(1)} %bitcast.200), kind=kOutput, calls=%fused_computation | convolution fusion | flops 1435385856 | bytes 6193152 | tf_op jit(solution)/shard_map/dot_general | solution.py:39
  69.7 4.1 %convolution_convert_fusion.1.q_ref.k_ref.v_ref = bf16[1664,768]{1,0:T(8,128)(2,1)S(1)} fusion(bf16[768,768]{1,0:T(8,128)(2,1)} %bitcast.36, bf16[384,768]{1,0:T(8,128)(2,1)S(1)} %copy-done.17, bf16[256,768]{1,0:T(8,128)(2,1)S(1)} %maximum_select_fusion.6, bf16[1024,768]{1,0:T(8,128)(2,1)S(1)} %copy-done.12), kind=kOutput, calls=%fused_computation.4 | convolution fusion | flops 1971879936 | bytes 6291456 | tf_op jit(solution)/shard_map/dot_general | solution.py:39
  73.8 15.9 %shard_map.332 = (bf16[1280,128]{1,0:T(8,128)(2,1)S(1)}, bf16[5,2,256,1408]{3,2,1,0:T(8,128)(2,1)}, f32[1280,128]{1,0:T(8,128)S(1)}) custom-call(s32[4]{0:T(128)S(1)} %bitcast.189, bf16[1664,768]{1,0:T(8,128)(2,1)S(1)} %convolution_convert_fusion.1.q_ref.k_ref.v_ref, bf16[1664,768]{1,0:T(8,128)(2,1)S(1)} %convolution_convert_fusion.1.q_ref.k_ref.v_ref, ...), custom_call_target="tpu_custom_call" | custom-call | flops 29527900160 | bytes 7208960 | tf_op jit(solution)/shard_map/pallas_call | solution.py:343
  90.4 16.0 %shard_map.333 = (bf16[1280,128]{1,0:T(8,128)(2,1)S(1)}, bf16[5,2,256,1408]{3,2,1,0:T(8,128)(2,1)}, f32[1280,128]{1,0:T(8,128)S(1)}) custom-call(s32[4]{0:T(128)S(1)} %bitcast.190, bf16[1664,768]{1,0:T(8,128)(2,1)S(1)} %convolution_convert_fusion.1.q_ref.k_ref.v_ref, bf16[1664,768]{1,0:T(8,128)(2,1)S(1)} %convolution_convert_fusion.1.q_ref.k_ref.v_ref, ...), custom_call_target="tpu_custom_call" | custom-call | flops 29527900160 | bytes 7208960 | tf_op jit(solution)/shard_map/pallas_call | solution.py:343
  107.2 1.5 convolution_convert_fusion.2.q_ref.k_ref.v_ref
  108.8 16.2 %shard_map.334 = (bf16[1280,128]{1,0:T(8,128)(2,1)S(1)}, bf16[5,2,256,1408]{3,2,1,0:T(8,128)(2,1)}, f32[1280,128]{1,0:T(8,128)S(1)}) custom-call(s32[4]{0:T(128)S(1)} %bitcast.191, bf16[1664,384]{1,0:T(8,128)(2,1)S(1)} %convolution_convert_fusion.2.q_ref.k_ref.v_ref, bf16[1664,384]{1,0:T(8,128)(2,1)S(1)} %convolution_convert_fusion.2.q_ref.k_ref.v_ref, ...), custom_call_target="tpu_custom_call" | custom-call | flops 29527900160 | bytes 7208960 | tf_op jit(solution)/shard_map/pallas_call | solution.py:343
  125.0 1.5 collective-permute-start.13
  128.0 4.1 %collective-permute-done.13 = bf16[640,128]{1,0:T(8,128)(2,1)S(1)} collective-permute-done((bf16[640,128]{1,0:T(8,128)(2,1)S(1)}, bf16[640,128]{1,0:T(8,128)(2,1)S(1)}, u32[]{:S(2)}, u32[]{:S(2)}) %collective-permute-start.13) | collective-permute-done | bytes 163872 | tf_op jit(solution)/shard_map/ppermute | solution.py:656
  132.2 2.2 collective-permute-done.14
  134.9 1.1 broadcast_select_fusion.attn_ref
  135.9 1.5 collective-permute-start.22
  138.1 1.0 slice_convert_fusion
  141.6 38.6 %shard_map.335 = (bf16[640,768]{1,0:T(8,128)(2,1)}, f32[640,768]{1,0:T(8,128)}, bf16[2,3,640,128]{3,2,1,0:T(8,128)(2,1)}, bf16[768,6912]{1,0:T(8,128)(2,1)}, f32[1,3072]{1,0:T(1,128)}, /*index=5*/f32[8,768]{1,0:T(8,128)}) custom-call(s32[1]{0:T(128)} %bitcast.side_ref, bf16[640,768]{1,0:T(8,128)(2,1)} %broadcast_select_fusion.attn_ref, ...), custom_call_target="tpu_custom_call" | custom-call | flops 18119393280 | bytes 47185920 | tf_op jit(solution)/shard_map/pallas_call | solution.py:611
  180.1 2.0 slice_bitcast_fusion.10
  183.8 0.9 slice_bitcast_fusion.1
  185.5 1.3 collective-permute-start.15
  188.4 1.3 collective-permute-start.19
  189.8 2.8 collective-permute-done.15
  192.8 22.0 %shard_map.336 = (bf16[1664,384]{1,0:T(8,128)(2,1)S(1)}, bf16[2432,128]{1,0:T(8,128)(2,1)S(1)}, f32[8,128]{1,0:T(8,128)S(1)}) custom-call(s32[4]{0:T(128)S(1)} %bitcast.192, bf16[1664,768]{1,0:T(8,128)(2,1)} %copy-done.3, bf16[1664,768]{1,0:T(8,128)(2,1)} %copy-done.3, bf16[1664,768]{1,0:T(8,128)(2,1)} %copy-done.3, bf16[2432,384]{1,0:T(8,128)(2,1)} %copy-done.1, ...), custom_call_target="tpu_custom_call" | custom-call | flops 44291850240 | bytes 7208960 | tf_op jit(solution)/shard_map/pallas_call | solution.py:374
  214.9 1.6 convolution_convert_fusion.5
  216.9 1.2 convolution_convert_fusion.9
  219.8 1.6 collective-permute-start.20
  223.3 6.1 %all-to-all-start = ((bf16[8,56,512]{2,1,0:T(8,128)(2,1)}), bf16[8,56,512]{2,1,0:T(8,128)(2,1)S(1)}, u32[]{:S(2)}, u32[]{:S(2)}) async-start(bf16[8,56,512]{2,1,0:T(8,128)(2,1)} %add_convert_fusion.2), calls=%async_computation | async-start | bytes 917504 | tf_op jit(solution)/shard_map/all_to_all | solution.py:924
  229.5 1.1 copy-done.5
  230.6 21.5 %shard_map.337 = (bf16[1664,384]{1,0:T(8,128)(2,1)S(1)}, bf16[2432,128]{1,0:T(8,128)(2,1)S(1)}, f32[8,128]{1,0:T(8,128)S(1)}) custom-call(s32[4]{0:T(128)S(1)} %bitcast.193, bf16[1664,768]{1,0:T(8,128)(2,1)} %copy-done.3, bf16[1664,768]{1,0:T(8,128)(2,1)} %copy-done.3, bf16[1664,768]{1,0:T(8,128)(2,1)} %copy-done.3, bf16[2432,384]{1,0:T(8,128)(2,1)} %copy-done.1, ...), custom_call_target="tpu_custom_call" | custom-call | flops 44291850240 | bytes 7208960 | tf_op jit(solution)/shard_map/pallas_call | solution.py:374
  253.8 3.4 convolution_convert_fusion.4
  257.3 1.2 convolution_convert_fusion.8
  258.9 2.8 collective-permute-start.21
  263.5 6.0 %all-to-all-start.1 = ((bf16[8,48,512]{2,1,0:T(8,128)(2,1)}), bf16[8,48,512]{2,1,0:T(8,128)(2,1)S(1)}, u32[]{:S(2)}, u32[]{:S(2)}) async-start(bf16[8,48,512]{2,1,0:T(8,128)(2,1)} %add_convert_fusion.3), calls=%async_computation.1 | async-start | bytes 786432 | tf_op jit(solution)/shard_map/all_to_all | solution.py:924
  269.7 1.1 copy-done.7
  270.8 21.3 %shard_map.338 = (bf16[1664,384]{1,0:T(8,128)(2,1)S(1)}, bf16[2432,128]{1,0:T(8,128)(2,1)S(1)}, f32[8,128]{1,0:T(8,128)S(1)}) custom-call(s32[4]{0:T(128)S(1)} %bitcast.194, bf16[1664,384]{1,0:T(8,128)(2,1)} %copy-done.2, bf16[1664,384]{1,0:T(8,128)(2,1)} %copy-done.2, bf16[1664,384]{1,0:T(8,128)(2,1)} %copy-done.2, bf16[2432,384]{1,0:T(8,128)(2,1)} %copy-done.1, ...), custom_call_target="tpu_custom_call" | custom-call | flops 44291850240 | bytes 7208960 | tf_op jit(solution)/shard_map/pallas_call | solution.py:374
  293.1 3.3 convolution_convert_fusion.3
  296.7 1.8 copy-done.10
  298.5 1.2 convolution_convert_fusion.7
  299.9 1.5 copy-done.29
  302.1 1.1 constant_dynamic-update-slice_fusion.24
  303.2 1.1 constant_dynamic-update-slice_fusion.23
  304.3 5.3 %fusion = f32[640,768]{1,0:T(8,128)} fusion(bf16[640,1920]{1,0:T(8,128)(2,1)S(1)} %constant_dynamic-update-slice_fusion.23, bf16[768,768]{1,0:T(8,128)(2,1)} %collective-permute-done.22, bf16[768,384]{1,0:T(8,128)(2,1)} %slice.393, bf16[768,768]{1,0:T(8,128)(2,1)} %bitcast.36), kind=kOutput, calls=%fused_computation.5 | convolution fusion | flops 1896284160 | bytes 7372800 | tf_op jit(solution)/shard_map/dot_general | solution.py:43
  310.5 6.0 %all-to-all-start.2 = ((bf16[8,56,512]{2,1,0:T(8,128)(2,1)}), bf16[8,56,512]{2,1,0:T(8,128)(2,1)S(1)}, u32[]{:S(2)}, u32[]{:S(2)}) async-start(bf16[8,56,512]{2,1,0:T(8,128)(2,1)} %add_convert_fusion.1), calls=%async_computation.2 | async-start | bytes 917504 | tf_op jit(solution)/shard_map/all_to_all | solution.py:924
  317.3 3.2 add_add_fusion
  320.5 1.2 slice_bitcast_fusion
  321.8 7.4 %reduce-scatter.2.cloned.1.call-done = bf16[48,6912]{1,0:T(8,128)(2,1)} async-done(((bf16[768,6912]{1,0:T(8,128)(2,1)}), bf16[48,6912]{1,0:T(8,128)(2,1)}) %reduce-scatter.2.cloned.1.call-update) | async-done | bytes 663568 | tf_op jit(solution)/shard_map/reduce_scatter | solution.py:881
  329.1 1.1 constant_dynamic-slice_fusion.4
  331.6 8.6 %collective-permute-done.26 = bf16[1,24,6912]{2,1,0:T(8,128)(2,1)} collective-permute-done((bf16[1,24,6912]{2,1,0:T(8,128)(2,1)S(1)}, bf16[1,24,6912]{2,1,0:T(8,128)(2,1)}, u32[]{:S(2)}, u32[]{:S(2)}) %collective-permute-start.26) | collective-permute-done | bytes 331808 | tf_op jit(solution)/shard_map/ppermute | solution.py:656
  340.2 1.0 pad_maximum_fusion.6
  342.0 1.8 collective-permute-start.27
  (345 shorter events, 54.0 us)
Async XLA Ops:
  7.2 131.0 %all-gather.2.cloned.1.call-start = ((), (), s32[]{:S(2)}) async-start(), calls=%async_computation.4 | async-start | bytes 11489280 | tf_op jit(solution)/shard_map/all_gather | solution.py:813
  11.6 19.4 %collective-permute-start = (bf16[48,768]{1,0:T(8,128)(2,1)S(1)}, bf16[48,768]{1,0:T(8,128)(2,1)S(1)}, u32[]{:S(2)}, u32[]{:S(2)}) collective-permute-start(bf16[48,768]{1,0:T(8,128)(2,1)S(1)} %constant_dynamic-update-slice_fusion), channel_id=1, source_target_pairs={{0,8},{1,9},{2,10},{3,11},{4,12},{5,13},{6,14},{7,15},{8,0},{9,1},... | collective-permute-start | bytes 221192 | tf_op jit(solution)/shard_map/ppermute | solution.py:665
  13.4 12.6 %copy-start.37 = (bf16[2,48]{1,0:T(2,128)(2,1)S(1)}, bf16[2,48]{1,0:T(2,128)(2,1)}, u32[]{:S(2)}) copy-start(bf16[2,48]{1,0:T(2,128)(2,1)} %param.38) | copy-start | bytes 580
  13.4 12.7 %copy-start.38 = (bf16[2,48]{1,0:T(2,128)(2,1)S(1)}, bf16[2,48]{1,0:T(2,128)(2,1)}, u32[]{:S(2)}) copy-start(bf16[2,48]{1,0:T(2,128)(2,1)} %param.39) | copy-start | bytes 580
  13.4 12.8 %slice-start.4 = ((s32[1,1408]{1,0:T(1,128)}), s32[1,1024]{1,0:T(1,128)S(1)}, s32[]{:S(2)}) async-start(s32[1,1408]{1,0:T(1,128)} %param.24), calls=%async_computation.10 | async-start | bytes 8192 | tf_op jit(solution)/shard_map/slice | solution.py:770
  13.5 17.5 %collective-permute-start.1 = (bf16[48,896]{1,0:T(8,128)(2,1)S(1)}, bf16[48,896]{1,0:T(8,128)(2,1)S(1)}, u32[]{:S(2)}, u32[]{:S(2)}) collective-permute-start(bf16[48,896]{1,0:T(8,128)(2,1)S(1)} %constant_dynamic-update-slice_fusion.6), channel_id=1, source_target_pairs={{0,2},{1,3},{2,0},{3,1},{4,6},{5,7},{6,4},{7,5},{8,10},{9,11},{10,... | collective-permute-start | bytes 258056 | tf_op jit(solution)/shard_map/ppermute | solution.py:665
  15.2 15.8 %collective-permute-start.2 = (bf16[256,768]{1,0:T(8,128)(2,1)S(1)}, bf16[256,768]{1,0:T(8,128)(2,1)S(1)}, u32[]{:S(2)}, u32[]{:S(2)}) collective-permute-start(bf16[256,768]{1,0:T(8,128)(2,1)S(1)} %get-tuple-element.149), channel_id=1, source_target_pairs={{0,16},{16,0},{1,17},{17,1},{2,18},{18,2},{3,19},{19,3},{4,20},{20... | collective-permute-start | bytes 1179656 | tf_op jit(solution)/shard_map/ppermute | solution.py:656
  15.8 20.1 %collective-permute-start.5 = (bf16[256,768]{1,0:T(8,128)(2,1)S(1)}, bf16[256,768]{1,0:T(8,128)(2,1)}, u32[]{:S(2)}, u32[]{:S(2)}) collective-permute-start(bf16[256,768]{1,0:T(8,128)(2,1)S(1)} %get-tuple-element.148), channel_id=1, source_target_pairs={{0,16},{16,0},{1,17},{17,1},{2,18},{18,2},{3,19},{19,3},{4,20},{20... | collective-permute-start | bytes 1179656 | tf_op jit(solution)/shard_map/ppermute | solution.py:656
  17.3 27.6 %collective-permute-start.8 = (bf16[192,768]{1,0:T(8,128)(2,1)}, bf16[192,768]{1,0:T(8,128)(2,1)}, u32[]{:S(2)}, u32[]{:S(2)}) collective-permute-start(bf16[192,768]{1,0:T(8,128)(2,1)} %bitcast.245), channel_id=1, source_target_pairs={{0,16},{16,0},{1,17},{17,1},{2,18},{18,2},{3,19},{19,3},{4,20},{20... | collective-permute-start | bytes 884744 | tf_op jit(solution)/shard_map/ppermute | solution.py:656
  30.9 13.1 %copy-start.30 = (bf16[48,768]{1,0:T(8,128)(2,1)S(1)}, bf16[48,768]{1,0:T(8,128)(2,1)}, u32[]{:S(2)}) copy-start(bf16[48,768]{1,0:T(8,128)(2,1)} %param.30) | copy-start | bytes 221188
  30.9 19.5 %copy-start.26 = (bf16[1,128,768]{2,1,0:T(8,128)(2,1)S(1)}, bf16[1,128,768]{2,1,0:T(8,128)(2,1)}, u32[]{:S(2)}) copy-start(bf16[1,128,768]{2,1,0:T(8,128)(2,1)} %param.22) | copy-start | bytes 589828
  31.0 10.2 %collective-permute-start.4 = (bf16[2,48,896]{2,1,0:T(8,128)(2,1)S(1)}, bf16[2,48,896]{2,1,0:T(8,128)(2,1)S(1)}, u32[]{:S(2)}, u32[]{:S(2)}) collective-permute-start(bf16[2,48,896]{2,1,0:T(8,128)(2,1)S(1)} %maximum_select_fusion.13), channel_id=1, source_target_pairs={{0,8},{1,9},{2,10},{3,11},{4,12},{5,13},{6,14},{7,15},{8,0},{9,1},... | collective-permute-start | bytes 516104 | tf_op jit(solution)/shard_map/ppermute | solution.py:665
  33.7 7.6 %collective-permute-start.3 = (bf16[2,48,768]{2,1,0:T(8,128)(2,1)S(1)}, bf16[2,48,768]{2,1,0:T(8,128)(2,1)S(1)}, u32[]{:S(2)}, u32[]{:S(2)}) collective-permute-start(bf16[2,48,768]{2,1,0:T(8,128)(2,1)S(1)} %maximum_select_fusion.15), channel_id=1, source_target_pairs={{0,4},{1,5},{2,6},{3,7},{4,0},{5,1},{6,2},{7,3},{8,12},{9,13},{10,... | collective-permute-start | bytes 442376 | tf_op jit(solution)/shard_map/ppermute | solution.py:665
  41.3 8.4 %collective-permute-start.7 = (bf16[2,2,48,896]{3,2,1,0:T(8,128)(2,1)S(1)}, bf16[2,2,48,896]{3,2,1,0:T(8,128)(2,1)S(1)}, u32[]{:S(2)}, u32[]{:S(2)}) collective-permute-start(bf16[2,2,48,896]{3,2,1,0:T(8,128)(2,1)S(1)} %maximum_select_fusion.7), channel_id=1, source_target_pairs={{0,4},{1,5},{2,6},{3,7},{4,0},{5,1},{6,2},{7,3},{8,12},{9,13},{10,... | collective-permute-start | bytes 1032200 | tf_op jit(solution)/shard_map/ppermute | solution.py:665
  42.5 7.1 %collective-permute-start.6 = (bf16[2,2,48,768]{3,2,1,0:T(8,128)(2,1)}, bf16[2,2,48,768]{3,2,1,0:T(8,128)(2,1)S(1)}, u32[]{:S(2)}, u32[]{:S(2)}) collective-permute-start(bf16[2,2,48,768]{3,2,1,0:T(8,128)(2,1)} %maximum_select_fusion.9), channel_id=1, source_target_pairs={{0,2},{1,3},{2,0},{3,1},{4,6},{5,7},{6,4},{7,5},{8,10},{9,11},{10,... | collective-permute-start | bytes 884744 | tf_op jit(solution)/shard_map/ppermute | solution.py:665
  44.9 8.2 %copy-start.11 = (bf16[1,512,768]{2,1,0:T(8,128)(2,1)S(1)}, bf16[1,512,768]{2,1,0:T(8,128)(2,1)}, u32[]{:S(2)}) copy-start(bf16[1,512,768]{2,1,0:T(8,128)(2,1)} %param.21) | copy-start | bytes 2359300
  49.8 279.4 %reduce-scatter.2.cloned.1.call-start = ((), (), s32[]{:S(2)}) async-start(), calls=%async_computation.5 | async-start | bytes 11280384 | tf_op jit(solution)/shard_map/reduce_scatter | solution.py:881
  50.4 9.9 %collective-permute-start.11 = (bf16[128,768]{1,0:T(8,128)(2,1)S(1)}, bf16[128,768]{1,0:T(8,128)(2,1)S(1)}, u32[]{:S(2)}, u32[]{:S(2)}) collective-permute-start(bf16[128,768]{1,0:T(8,128)(2,1)S(1)} %bitcast.252), channel_id=1, source_target_pairs={{0,16},{16,0},{1,17},{17,1},{2,18},{18,2},{3,19},{19,3},{4,20},{20... | collective-permute-start | bytes 589832 | tf_op jit(solution)/shard_map/ppermute | solution.py:656
  56.2 4.1 %collective-permute-start.10 = (bf16[2,2,2,48,896]{4,3,2,1,0:T(8,128)(2,1)S(1)}, bf16[2,2,2,48,896]{4,3,2,1,0:T(8,128)(2,1)S(1)}, u32[]{:S(2)}, u32[]{:S(2)}) collective-permute-start(bf16[2,2,2,48,896]{4,3,2,1,0:T(8,128)(2,1)S(1)} %maximum_select_fusion.3), channel_id=1, source_target_pairs={{0,1},{1,0},{2,3},{3,2},{4,5},{5,4},{6,7},{7,6},{8,9},{9,8},{10,11... | collective-permute-start | bytes 2064392 | tf_op jit(solution)/shard_map/ppermute | solution.py:665
  56.5 3.9 %collective-permute-start.9 = (bf16[2,2,2,48,768]{4,3,2,1,0:T(8,128)(2,1)S(1)}, bf16[2,2,2,48,768]{4,3,2,1,0:T(8,128)(2,1)S(1)}, u32[]{:S(2)}, u32[]{:S(2)}) collective-permute-start(bf16[2,2,2,48,768]{4,3,2,1,0:T(8,128)(2,1)S(1)} %maximum_select_fusion.4), channel_id=1, source_target_pairs={{0,1},{1,0},{2,3},{3,2},{4,5},{5,4},{6,7},{7,6},{8,9},{9,8},{10,11... | collective-permute-start | bytes 1769480 | tf_op jit(solution)/shard_map/ppermute | solution.py:665
  58.1 3.4 copy-start.27
  62.7 44.6 %copy-start.22 = (bf16[256,768]{1,0:T(8,128)(2,1)}, bf16[256,768]{1,0:T(8,128)(2,1)S(1)}, u32[]{:S(2)}) copy-start(bf16[256,768]{1,0:T(8,128)(2,1)S(1)} %maximum_select_fusion.6) | copy-start | bytes 1179652
  65.3 4.4 %copy-start.12 = (bf16[1024,768]{1,0:T(8,128)(2,1)S(1)}, bf16[1024,768]{1,0:T(8,128)(2,1)}, u32[]{:S(2)}) copy-start(bf16[1024,768]{1,0:T(8,128)(2,1)} %maximum_select_fusion) | copy-start | bytes 4718596
  65.3 4.4 %copy-start.17 = (bf16[384,768]{1,0:T(8,128)(2,1)S(1)}, bf16[384,768]{1,0:T(8,128)(2,1)}, u32[]{:S(2)}) copy-start(bf16[384,768]{1,0:T(8,128)(2,1)} %maximum_select_fusion.5) | copy-start | bytes 1769476
  69.6 39.1 %copy-start.1 = (bf16[2432,384]{1,0:T(8,128)(2,1)}, bf16[2432,384]{1,0:T(8,128)(2,1)S(1)}, u32[]{:S(2)}) copy-start(bf16[2432,384]{1,0:T(8,128)(2,1)S(1)} %convolution_convert_fusion.rel_ref) | copy-start | bytes 5603332
  69.6 4.1 %copy-start = (s32[1,4]{1,0:T(1,128)S(1)}, s32[1,4]{1,0:T(1,128)}, u32[]{:S(2)}) copy-start(s32[1,4]{1,0:T(1,128)} %param.25) | copy-start | bytes 52
  73.8 16.6 %copy-start.3 = (bf16[1664,768]{1,0:T(8,128)(2,1)}, bf16[1664,768]{1,0:T(8,128)(2,1)S(1)}, u32[]{:S(2)}) copy-start(bf16[1664,768]{1,0:T(8,128)(2,1)S(1)} %convolution_convert_fusion.1.q_ref.k_ref.v_ref) | copy-start | bytes 7667716
  89.8 38.2 %collective-permute-start.12 = (bf16[640,128]{1,0:T(8,128)(2,1)S(1)}, bf16[640,128]{1,0:T(8,128)(2,1)S(1)}, u32[]{:S(2)}, u32[]{:S(2)}) collective-permute-start(bf16[640,128]{1,0:T(8,128)(2,1)S(1)} %pad_maximum_fusion.22), channel_id=1, source_target_pairs={{0,16},{16,0},{1,17},{17,1},{2,18},{18,2},{3,19},{19,3},{4,20},{20... | collective-permute-start | bytes 491528 | tf_op jit(solution)/shard_map/ppermute | solution.py:656
  108.7 16.2 %copy-start.2 = (bf16[1664,384]{1,0:T(8,128)(2,1)}, bf16[1664,384]{1,0:T(8,128)(2,1)S(1)}, u32[]{:S(2)}) copy-start(bf16[1664,384]{1,0:T(8,128)(2,1)S(1)} %convolution_convert_fusion.2.q_ref.k_ref.v_ref) | copy-start | bytes 3833860
  125.0 9.8 %copy-start.6 = (f32[1280,128]{1,0:T(8,128)}, f32[1280,128]{1,0:T(8,128)S(1)}, u32[]{:S(2)}) copy-start(f32[1280,128]{1,0:T(8,128)S(1)} %get-tuple-element.111.inv_ref) | copy-start | bytes 1966084
  125.0 7.2 %collective-permute-start.13 = (bf16[640,128]{1,0:T(8,128)(2,1)S(1)}, bf16[640,128]{1,0:T(8,128)(2,1)S(1)}, u32[]{:S(2)}, u32[]{:S(2)}) collective-permute-start(bf16[640,128]{1,0:T(8,128)(2,1)S(1)} %pad_maximum_fusion.23), channel_id=1, source_target_pairs={{0,16},{16,0},{1,17},{17,1},{2,18},{18,2},{3,19},{19,3},{4,20},{20... | collective-permute-start | bytes 491528 | tf_op jit(solution)/shard_map/ppermute | solution.py:656
  127.4 7.0 %collective-permute-start.14 = (bf16[640,128]{1,0:T(8,128)(2,1)S(1)}, bf16[640,128]{1,0:T(8,128)(2,1)S(1)}, u32[]{:S(2)}, u32[]{:S(2)}) collective-permute-start(bf16[640,128]{1,0:T(8,128)(2,1)S(1)} %pad_maximum_fusion.24), channel_id=1, source_target_pairs={{0,16},{16,0},{1,17},{17,1},{2,18},{18,2},{3,19},{19,3},{4,20},{20... | collective-permute-start | bytes 491528 | tf_op jit(solution)/shard_map/ppermute | solution.py:656
  135.9 168.4 %collective-permute-start.22 = (bf16[768,768]{1,0:T(8,128)(2,1)}, bf16[768,768]{1,0:T(8,128)(2,1)}, u32[]{:S(2)}, u32[]{:S(2)}) collective-permute-start(bf16[768,768]{1,0:T(8,128)(2,1)} %bitcast.36), channel_id=1, source_target_pairs={{0,16},{16,0},{1,17},{17,1},{2,18},{18,2},{3,19},{19,3},{4,20},{20... | collective-permute-start | bytes 3538952 | tf_op jit(solution)/shard_map/ppermute | solution.py:656
  137.4 179.1 %collective-permute-start.24 = (bf16[768,384]{1,0:T(8,128)(2,1)}, bf16[768,384]{1,0:T(8,128)(2,1)}, u32[]{:S(2)}, u32[]{:S(2)}) collective-permute-start(bf16[768,384]{1,0:T(8,128)(2,1)} %slice.393), channel_id=1, source_target_pairs={{0,16},{16,0},{1,17},{17,1},{2,18},{18,2},{3,19},{19,3},{4,20},{20... | collective-permute-start | bytes 1769480 | tf_op jit(solution)/shard_map/ppermute | solution.py:656
  180.1 3.7 %copy-start.14 = (bf16[640,768]{1,0:T(8,128)(2,1)S(1)}, bf16[640,768]{1,0:T(8,128)(2,1)}, u32[]{:S(2)}) copy-start(bf16[640,768]{1,0:T(8,128)(2,1)} %get-tuple-element.92) | copy-start | bytes 2949124
  185.5 7.1 %collective-permute-start.15 = (bf16[640,128]{1,0:T(8,128)(2,1)S(1)}, bf16[640,128]{1,0:T(8,128)(2,1)S(1)}, u32[]{:S(2)}, u32[]{:S(2)}) collective-permute-start(bf16[640,128]{1,0:T(8,128)(2,1)S(1)} %get-tuple-element.143), channel_id=1, source_target_pairs={{0,16},{16,0},{1,17},{17,1},{2,18},{18,2},{3,19},{19,3},{4,20},{20... | collective-permute-start | bytes 491528 | tf_op jit(solution)/shard_map/ppermute | solution.py:656
  187.6 32.2 %collective-permute-start.17 = (bf16[640,128]{1,0:T(8,128)(2,1)S(1)}, bf16[640,128]{1,0:T(8,128)(2,1)S(1)}, u32[]{:S(2)}, u32[]{:S(2)}) collective-permute-start(bf16[640,128]{1,0:T(8,128)(2,1)S(1)} %get-tuple-element.146), channel_id=1, source_target_pairs={{0,16},{16,0},{1,17},{17,1},{2,18},{18,2},{3,19},{19,3},{4,20},{20... | collective-permute-start | bytes 491528 | tf_op jit(solution)/shard_map/ppermute | solution.py:656
  188.4 33.0 %collective-permute-start.19 = (bf16[640,128]{1,0:T(8,128)(2,1)S(1)}, bf16[640,128]{1,0:T(8,128)(2,1)S(1)}, u32[]{:S(2)}, u32[]{:S(2)}) collective-permute-start(bf16[640,128]{1,0:T(8,128)(2,1)S(1)} %get-tuple-element.144), channel_id=1, source_target_pairs={{0,16},{16,0},{1,17},{17,1},{2,18},{18,2},{3,19},{19,3},{4,20},{20... | collective-permute-start | bytes 491528 | tf_op jit(solution)/shard_map/ppermute | solution.py:656
  192.8 22.1 %copy-start.13 = (bf16[1024,768]{1,0:T(8,128)(2,1)S(1)}, bf16[1024,768]{1,0:T(8,128)(2,1)}, u32[]{:S(2)}) copy-start(bf16[1024,768]{1,0:T(8,128)(2,1)} %maximum_select_fusion) | copy-start | bytes 4718596
  192.8 22.1 %copy-start.18 = (bf16[384,768]{1,0:T(8,128)(2,1)S(1)}, bf16[384,768]{1,0:T(8,128)(2,1)}, u32[]{:S(2)}) copy-start(bf16[384,768]{1,0:T(8,128)(2,1)} %maximum_select_fusion.5) | copy-start | bytes 1769476
  192.8 22.1 %copy-start.23 = (bf16[256,768]{1,0:T(8,128)(2,1)S(1)}, bf16[256,768]{1,0:T(8,128)(2,1)}, u32[]{:S(2)}) copy-start(bf16[256,768]{1,0:T(8,128)(2,1)} %copy-done.22) | copy-start | bytes 1179652
  218.2 4.2 %collective-permute-start.16 = (bf16[8,56,512]{2,1,0:T(8,128)(2,1)S(1)}, bf16[8,56,512]{2,1,0:T(8,128)(2,1)S(1)}, u32[]{:S(2)}, u32[]{:S(2)}) collective-permute-start(bf16[8,56,512]{2,1,0:T(8,128)(2,1)S(1)} %pad_maximum_fusion.13), channel_id=1, source_target_pairs={{0,1},{1,0},{2,3},{3,2},{4,5},{5,4},{6,7},{7,6},{8,9},{9,8},{10,11... | collective-permute-start | bytes 1376264 | tf_op jit(solution)/shard_map/ppermute | solution.py:665
  219.8 81.7 %collective-permute-start.20 = (bf16[640,384]{1,0:T(8,128)(2,1)}, bf16[640,384]{1,0:T(8,128)(2,1)}, u32[]{:S(2)}, u32[]{:S(2)}) collective-permute-start(bf16[640,384]{1,0:T(8,128)(2,1)} %pad_maximum_fusion.10), channel_id=1, source_target_pairs={{0,16},{16,0},{1,17},{17,1},{2,18},{18,2},{3,19},{19,3},{4,20},{20... | collective-permute-start | bytes 1474568 | tf_op jit(solution)/shard_map/ppermute | solution.py:656
  221.5 8.0 %copy-start.19 = (bf16[640,128]{1,0:T(8,128)(2,1)}, bf16[640,128]{1,0:T(8,128)(2,1)S(1)}, u32[]{:S(2)}) copy-start(bf16[640,128]{1,0:T(8,128)(2,1)S(1)} %collective-permute-done.19) | copy-start | bytes 491524
  223.3 29.8 %all-to-all-start = ((bf16[8,56,512]{2,1,0:T(8,128)(2,1)}), bf16[8,56,512]{2,1,0:T(8,128)(2,1)S(1)}, u32[]{:S(2)}, u32[]{:S(2)}) async-start(bf16[8,56,512]{2,1,0:T(8,128)(2,1)} %add_convert_fusion.2), calls=%async_computation | async-start | bytes 917504 | tf_op jit(solution)/shard_map/all_to_all | solution.py:924
  253.7 3.5 copy-start.9
  258.6 4.0 %collective-permute-start.18 = (bf16[8,48,512]{2,1,0:T(8,128)(2,1)S(1)}, bf16[8,48,512]{2,1,0:T(8,128)(2,1)S(1)}, u32[]{:S(2)}, u32[]{:S(2)}) collective-permute-start(bf16[8,48,512]{2,1,0:T(8,128)(2,1)S(1)} %pad_maximum_fusion.15), channel_id=1, source_target_pairs={{0,1},{1,0},{2,3},{3,2},{4,5},{5,4},{6,7},{7,6},{8,9},{9,8},{10,11... | collective-permute-start | bytes 1179656 | tf_op jit(solution)/shard_map/ppermute | solution.py:665
  258.7 4.8 %copy-start.15 = (bf16[640,128]{1,0:T(8,128)(2,1)S(1)}, bf16[640,128]{1,0:T(8,128)(2,1)}, u32[]{:S(2)}) copy-start(bf16[640,128]{1,0:T(8,128)(2,1)} %get-tuple-element.110) | copy-start | bytes 491524
  258.8 10.7 %slice-start.1 = ((bf16[640,128]{1,0:T(8,128)(2,1)}), bf16[128,128]{1,0:T(8,128)(2,1)S(1)}, s32[]{:S(2)}) async-start(bf16[640,128]{1,0:T(8,128)(2,1)} %copy-done.19), calls=%async_computation.7 | async-start | bytes 65536 | tf_op jit(solution)/shard_map/slice | solution.py:940
  258.9 10.7 %slice-start = ((bf16[640,128]{1,0:T(8,128)(2,1)}), bf16[512,128]{1,0:T(8,128)(2,1)S(1)}, s32[]{:S(2)}) async-start(bf16[640,128]{1,0:T(8,128)(2,1)} %copy-done.19), calls=%async_computation.6 | async-start | bytes 262144 | tf_op jit(solution)/shard_map/slice | solution.py:940
  258.9 44.3 %collective-permute-start.21 = (bf16[640,384]{1,0:T(8,128)(2,1)S(1)}, bf16[640,384]{1,0:T(8,128)(2,1)}, u32[]{:S(2)}, u32[]{:S(2)}) collective-permute-start(bf16[640,384]{1,0:T(8,128)(2,1)S(1)} %pad_maximum_fusion.11), channel_id=1, source_target_pairs={{0,16},{16,0},{1,17},{17,1},{2,18},{18,2},{3,19},{19,3},{4,20},{20... | collective-permute-start | bytes 1474568 | tf_op jit(solution)/shard_map/ppermute | solution.py:656
  263.5 28.9 %all-to-all-start.1 = ((bf16[8,48,512]{2,1,0:T(8,128)(2,1)}), bf16[8,48,512]{2,1,0:T(8,128)(2,1)S(1)}, u32[]{:S(2)}, u32[]{:S(2)}) async-start(bf16[8,48,512]{2,1,0:T(8,128)(2,1)} %add_convert_fusion.3), calls=%async_computation.1 | async-start | bytes 786432 | tf_op jit(solution)/shard_map/all_to_all | solution.py:924
  270.8 21.3 %copy-start.32 = (bf16[8,128]{1,0:T(8,128)(2,1)S(1)}, bf16[8,128]{1,0:T(8,128)(2,1)}, u32[]{:S(2)}) copy-start(bf16[8,128]{1,0:T(8,128)(2,1)} %convert.46) | copy-start | bytes 6148
  270.8 21.4 %copy-start.33 = (bf16[8,128]{1,0:T(8,128)(2,1)S(1)}, bf16[8,128]{1,0:T(8,128)(2,1)}, u32[]{:S(2)}) copy-start(bf16[8,128]{1,0:T(8,128)(2,1)} %convert.47) | copy-start | bytes 6148
  299.8 9.9 %collective-permute-start.25 = (bf16[8,56,512]{2,1,0:T(8,128)(2,1)S(1)}, bf16[8,56,512]{2,1,0:T(8,128)(2,1)S(1)}, u32[]{:S(2)}, u32[]{:S(2)}) collective-permute-start(bf16[8,56,512]{2,1,0:T(8,128)(2,1)S(1)} %pad_maximum_fusion.14), channel_id=1, source_target_pairs={{0,1},{1,0},{2,3},{3,2},{4,5},{5,4},{6,7},{7,6},{8,9},{9,8},{10,11... | collective-permute-start | bytes 1376264 | tf_op jit(solution)/shard_map/ppermute | solution.py:665
  301.5 15.0 %collective-permute-start.23 = (bf16[640,384]{1,0:T(8,128)(2,1)S(1)}, bf16[640,384]{1,0:T(8,128)(2,1)S(1)}, u32[]{:S(2)}, u32[]{:S(2)}) collective-permute-start(bf16[640,384]{1,0:T(8,128)(2,1)S(1)} %pad_maximum_fusion.12), channel_id=1, source_target_pairs={{0,16},{16,0},{1,17},{17,1},{2,18},{18,2},{3,19},{19,3},{4,20},{20... | collective-permute-start | bytes 1474568 | tf_op jit(solution)/shard_map/ppermute | solution.py:656
  310.5 21.0 %all-to-all-start.2 = ((bf16[8,56,512]{2,1,0:T(8,128)(2,1)}), bf16[8,56,512]{2,1,0:T(8,128)(2,1)S(1)}, u32[]{:S(2)}, u32[]{:S(2)}) async-start(bf16[8,56,512]{2,1,0:T(8,128)(2,1)} %add_convert_fusion.1), calls=%async_computation.2 | async-start | bytes 917504 | tf_op jit(solution)/shard_map/all_to_all | solution.py:924
  321.8 19.5 %copy-start.21 = (f32[56,512]{1,0:T(8,128)S(1)}, f32[56,512]{1,0:T(8,128)}, u32[]{:S(2)}) copy-start(f32[56,512]{1,0:T(8,128)} %convert_reduce_fusion.2) | copy-start | bytes 344068
  330.3 11.7 %slice-start.3 = ((f32[48,512]{1,0:T(8,128)}), f32[48,384]{1,0:T(8,128)S(1)}, s32[]{:S(2)}) async-start(f32[48,512]{1,0:T(8,128)} %convert_reduce_fusion.3), calls=%async_computation.9 | async-start | bytes 147456 | tf_op jit(solution)/shard_map/slice | solution.py:983
  330.3 10.0 %collective-permute-start.26 = (bf16[1,24,6912]{2,1,0:T(8,128)(2,1)S(1)}, bf16[1,24,6912]{2,1,0:T(8,128)(2,1)}, u32[]{:S(2)}, u32[]{:S(2)}) collective-permute-start(bf16[1,24,6912]{2,1,0:T(8,128)(2,1)S(1)} %get-tuple-element.153), channel_id=1, source_target_pairs={{0,16},{16,0},{1,17},{17,1},{2,18},{18,2},{3,19},{19,3},{4,20},{20... | collective-permute-start | bytes 995336 | tf_op jit(solution)/shard_map/ppermute | solution.py:656
  341.3 3.2 copy-start.25
  341.5 3.5 slice-start.2
  341.6 7.5 %collective-permute-start.28 = (bf16[512]{0:T(512)(128)(2,1)S(1)}, bf16[512]{0:T(512)(128)(2,1)S(1)}, u32[]{:S(2)}, u32[]{:S(2)}) collective-permute-start(bf16[512]{0:T(512)(128)(2,1)S(1)} %fusion.35), channel_id=1, source_target_pairs={{0,16},{16,0},{1,17},{17,1},{2,18},{18,2},{3,19},{19,3},{4,20},{20... | collective-permute-start | bytes 3080 | tf_op jit(solution)/shard_map/ppermute | solution.py:656
  342.0 9.5 %collective-permute-start.27 = (bf16[24,1152]{1,0:T(8,128)(2,1)S(1)}, bf16[24,1152]{1,0:T(8,128)(2,1)S(1)}, u32[]{:S(2)}, u32[]{:S(2)}) collective-permute-start(bf16[24,1152]{1,0:T(8,128)(2,1)S(1)} %dynamic-slice_convert_fusion), channel_id=1, source_target_pairs={{0,16},{16,0},{1,17},{17,1},{2,18},{18,2},{3,19},{19,3},{4,20},{20... | collective-permute-start | bytes 165896 | tf_op jit(solution)/shard_map/ppermute | solution.py:656
  (14 other events, 19.8 us)
Sparse Core Ops, SparseCore 0:
  49.9 88.2 all-gather.1
  185.6 143.4 reduce-scatter.1
where the time goes:
time: 367 us; the launch traced here: 361 us
  Pallas kernels  152 us (41%)
  starting transfers between devices  45.1 us (12%)
  local copies, waits for them, and re-layouts  43.1 us (12%)
  waiting for transfers between devices  38 us (10%)
  other arithmetic  34.3 us (9%)
  matrix products  32.2 us (9%)
  between operations  16.5 us (4%)
    pallas_call x3, Pallas kernels, attention_backward(): pl.pallas_call(backward_kernel, grid_spec=pltpu.PrefetchScalarGridSpec(nu...  64.9 us
    pallas_call x3, Pallas kernels, attention_forward(): pl.pallas_call(forward_kernel, grid_spec=pltpu.PrefetchScalarGridSpec(num...  48.1 us
    pallas_call x1, Pallas kernels, middle(): pl.pallas_call(functools.partial(middle_kernel, groups), grid_spec=pltpu....  38.6 us
    ppermute x18, starting transfers between devices, swap(): return lax.ppermute(values, 'seq', [(0, 1), (1, 0)])  19.5 us
    ppermute x18, waiting for transfers between devices, swap(): return lax.ppermute(values, 'seq', [(0, 1), (1, 0)])  19.4 us
    all_to_all x3, starting transfers between devices, sum_message(): lax.all_to_all(message, 'fsdp', split_axis=0, concat_axis=0, tiled=True,...  18.1 us
    unnamed x103, local copies, waits for them, and re-layouts  15.4 us
    dot_general x6, matrix products, inner_cols(): lax.dot_general(left, right, (((0,), (0,)), ((), ())), preferred_element_...  11.9 us
  transfers between devices with their start and end apart: 34, of which 12 were waited for; matrix products, arithmetic and copies ran while one was open for 26% of the time, Pallas kernels for 42%

commit v1 on v0

--- a/solution.py
+++ b/solution.py
@@ -191,7 +191,8 @@
     rel_ref,
     kx_ref,
     par_ref,
-    grad_ref,
+    near_ref,
+    far_ref,
     att_ref,
     inv_ref,
     exp_ref,
@@ -212,6 +213,7 @@
     accr_ref,
     span_ref,
     moved_ref,
+    grad_ref,
 ):
     step = pl.program_id(0)
 
@@ -222,6 +224,12 @@
         gather_keys(order_ref, v_ref, vcat_ref, slice(0, LANES))
         vcat_ref[:, :LANES] = (vcat_ref[:, :LANES].astype(F32) * SCORE_SCALE).astype(BF)
         vcat_ref[:, LANES:] = jnp.full((KEYS, LANES), SCORE_SCALE, BF)
+        half, part = L // 2, BLOCK // 2
+        for from_ref, which in ((near_ref, order_ref[NBLK]), (far_ref, 1 - order_ref[NBLK])):
+            rows_at = pl.multiple_of(which * half, half)
+            grad_ref[pl.ds(rows_at, half), :] = from_ref[:half, :]
+            rows_at = pl.multiple_of(QROW + which * part, part)
+            grad_ref[pl.ds(rows_at, part), :] = from_ref[half:, :]
         up = lax.broadcasted_iota(jnp.int32, (BLOCK, BLOCK), 0)
         down = lax.broadcasted_iota(jnp.int32, (BLOCK, BLOCK), 1)
         flip_ref[...] = jnp.where(up + down == BLOCK - 1, 1.0, 0.0).astype(BF)
@@ -366,8 +374,9 @@
     )(order, qkv, qkv, qkv, rel, marks, par)
 
 
-def attention_backward(pair, first, order, qkv, rel, marks, par, grad, att, inverse, exps_in):
+def attention_backward(pair, first, order, qkv, rel, marks, par, side, near, far, att, inverse, exps_in):
     ins, exps = attention_specs(pair, first)
+    order = jnp.concatenate([order, side.astype(order.dtype)[None]])
     qkv, rel, exps_in = (
         pltpu.with_memory_space_constraint(t, pltpu.HBM) for t in (qkv, rel, exps_in)
     )
@@ -376,7 +385,10 @@
         grid_spec=pltpu.PrefetchScalarGridSpec(
             num_scalar_prefetch=1,
             grid=(STEPS,),
-            in_specs=ins + [column(MROW, 0)] * 3 + [exps],
+            in_specs=ins
+            + [column(near.shape[0], 0)] * 2
+            + [column(MROW, 0)] * 2
+            + [exps],
             out_specs=[
                 pl.BlockSpec((ROWS, 3 * LANES), lambda step, order: (0, 0)),
                 column(REL_ROWS, 0),
@@ -397,6 +409,7 @@
                 pltpu.VMEM((2, BLOCK, LANES), F32),
                 pltpu.VMEM((SPANS, LANES), BF),
                 pltpu.VMEM((2, BLOCK, SPANS), BF),
+                pltpu.VMEM((MROW, LANES), BF),
             ],
         ),
         out_shape=[
@@ -405,7 +418,7 @@
             jax.ShapeDtypeStruct((8, LANES), F32),
         ],
         **settings(24),
-    )(order, qkv, qkv, qkv, rel, marks, par, grad, att, inverse, exps_in)
+    )(order, qkv, qkv, qkv, rel, marks, par, near, far, att, inverse, exps_in)
 
 
 CHUNKS = 2
@@ -448,10 +461,53 @@
     small_ref,
     result_ref,
     grad_sum_ref,
-    grad_attn_ref,
     gw_ref,
     gb_inner_ref,
     g_small_ref,
+    *rest,
+):
+    pairs = attn_ref.shape[1] // (2 * LANES)
+    near_refs, far_refs, rest = rest[:pairs], rest[pairs : 2 * pairs], rest[2 * pairs :]
+    middle_steps(
+        groups,
+        side_ref,
+        attn_ref,
+        hidden_ref,
+        query_ref,
+        grad_hidden_ref,
+        grad_query_ref,
+        weights_ref,
+        inner_bias_ref,
+        small_ref,
+        result_ref,
+        grad_sum_ref,
+        gw_ref,
+        gb_inner_ref,
+        g_small_ref,
+        near_refs,
+        far_refs,
+        *rest,
+    )
+
+
+def middle_steps(
+    groups,
+    side_ref,
+    attn_ref,
+    hidden_ref,
+    query_ref,
+    grad_hidden_ref,
+    grad_query_ref,
+    weights_ref,
+    inner_bias_ref,
+    small_ref,
+    result_ref,
+    grad_sum_ref,
+    gw_ref,
+    gb_inner_ref,
+    g_small_ref,
+    near_refs,
+    far_refs,
     unit_ref,
     scale_ref,
     low_ref,
@@ -576,8 +632,8 @@
         middle_at = width // 2
         for at in range(0, middle_at, LANES):
             near, far = back[:, at : at + LANES], back[:, middle_at + at :][:, :LANES]
-            grad_attn_ref[0, at // LANES] = jnp.where(left, near, far)
-            grad_attn_ref[1, at // LANES] = jnp.where(left, far, near)
+            near_refs[at // LANES][...] = jnp.where(left, near, far)
+            far_refs[at // LANES][...] = jnp.where(left, far, near)
 
 
 def middle(groups, side, attn, hidden, query, grad_hidden, grad_query, weights, inner_bias, small):
@@ -603,11 +659,10 @@
     outs = [
         jax.ShapeDtypeStruct((rows, width), BF),
         jax.ShapeDtypeStruct((rows, width), F32),
-        jax.ShapeDtypeStruct((2, width // 2 // LANES, rows, LANES), BF),
         jax.ShapeDtypeStruct((width, (1 + 2 * tiles) * width), BF),
         jax.ShapeDtypeStruct((1, tiles * width), F32),
         jax.ShapeDtypeStruct((8, width), F32),
-    ]
+    ] + [jax.ShapeDtypeStruct((rows, LANES), BF)] * (width // LANES)
     return pl.pallas_call(
         functools.partial(middle_kernel, groups),
         grid_spec=pltpu.PrefetchScalarGridSpec(
@@ -619,12 +674,13 @@
                 pl.BlockSpec((1, width), lambda step, side: (0, tile(step))),
                 whole(small),
             ],
-            out_specs=[whole(t) for t in outs[:3]]
+            out_specs=[whole(t) for t in outs[:2]]
             + [
                 square(written),
                 pl.BlockSpec((1, width), lambda step, side: (0, back(step))),
-                whole(outs[5]),
-            ],
+                whole(outs[4]),
+            ]
+            + [whole(t) for t in outs[5:]],
             scratch_shapes=[
                 pltpu.VMEM((rows, width), F32),
                 pltpu.VMEM((rows, LANES), F32),
@@ -864,7 +920,7 @@
     devices = 2 * groups
     out_rows = width // devices
     dealt_rows = out_rows % 8 == 0
-    result, grad_sum_one, grad_attn, grad_weights, grad_b_inner, grad_small = middle(
+    result, grad_sum_one, grad_weights, grad_b_inner, grad_small, *grad_attn = middle(
         groups if dealt_rows else None,
         side.astype(jnp.int32)[None],
         attn_rows,
@@ -904,7 +960,7 @@
     )
     far_one, far_two = swap(weights_one), swap(weights_two)
 
-    far_grads = [swap(grad_attn[1, pair]) for pair in range(pairs)]
+    far_grads = [swap(grad_attn[pairs + pair]) for pair in range(pairs)]
 
     core = place_at % 2
     same_core = [[at for at in range(groups) if at % 2 == which] for which in range(2)]
@@ -933,12 +989,11 @@
 
     own_rows_grads, far_rows_grads, sums, few_grads = [], [], [], []
     for pair in range(pairs):
-        own, far = grad_attn[0, pair], far_grads[pair]
+        own, far = grad_attn[pair], far_grads[pair]
         if pair:
             own, message, sums = lax.optimization_barrier((own, message, sums))
             sums.append(sum_message(message))
-        head_grad = jnp.concatenate([by_side(own[a:b], far[a:b], 0) for a, b in cuts], 0)
-        dqkv, drel, dpar = attention_backward(*pair_args(pair), head_grad, *kept[pair])
+        dqkv, drel, dpar = attention_backward(*pair_args(pair), side, own, far, *kept[pair])
         if pair:
             dqkv, drel, sums = lax.optimization_barrier((dqkv, drel, sums))
         few_grads.append(dpar[:5])

time: 367 us -> 362 us (0.986)
  the two profiles are of different devices: /device:TPU:30 before, /device:TPU:0 now
where the time goes in v1:
time: 362 us; the launch traced here: 356 us
  Pallas kernels  151 us (42%)
  starting transfers between devices  44.2 us (12%)
  local copies, waits for them, and re-layouts  41.9 us (12%)
  waiting for transfers between devices  35.7 us (10%)
  other arithmetic  33.8 us (9%)
  matrix products  32.1 us (9%)
  between operations  16.5 us (5%)
    pallas_call x3, Pallas kernels, attention_backward(): pl.pallas_call(backward_kernel, grid_spec=pltpu.PrefetchScalarGridSpec(nu...  64.6 us
    pallas_call x3, Pallas kernels, attention_forward(): pl.pallas_call(forward_kernel, grid_spec=pltpu.PrefetchScalarGridSpec(num...  48.2 us
    pallas_call x1, Pallas kernels, middle(): pl.pallas_call(functools.partial(middle_kernel, groups), grid_spec=pltpu....  38.6 us
    ppermute x18, starting transfers between devices, swap(): return lax.ppermute(values, 'seq', [(0, 1), (1, 0)])  20 us
    unnamed x107, local copies, waits for them, and re-layouts  16.3 us
    all_to_all x3, starting transfers between devices, sum_message(): lax.all_to_all(message, 'fsdp', split_axis=0, concat_axis=0, tiled=True,...  14.7 us
    ppermute x18, waiting for transfers between devices, swap(): return lax.ppermute(values, 'seq', [(0, 1), (1, 0)])  13.2 us
    dot_general x6, matrix products, inner_cols(): lax.dot_general(left, right, (((0,), (0,)), ((), ())), preferred_element_...  11.9 us
  transfers between devices with their start and end apart: 34, of which 12 were waited for; matrix products, arithmetic and copies ran while one was open for 25% of the time, Pallas kernels for 43%

profile of v1, /device:TPU:0, one launch (start us, length us, event | category | flops | bytes accessed | tf_op | source)
XLA Modules:
  0.0 355.7 jit_solution(8707693652835410720)
XLA Ops:
  11.6 4.0 %collective-permute-start = (bf16[48,768]{1,0:T(8,128)(2,1)S(1)}, bf16[48,768]{1,0:T(8,128)(2,1)S(1)}, u32[]{:S(2)}, u32[]{:S(2)}) collective-permute-start(bf16[48,768]{1,0:T(8,128)(2,1)S(1)} %constant_dynamic-update-slice_fusion), channel_id=1, source_target_pairs={{0,8},{1,9},{2,10},{3,11},{4,12},{5,13},{6,14},{7,15},{8,0},{9,1},... | collective-permute-start | bytes 221192 | tf_op jit(solution)/shard_map/ppermute | solution.py:721
  17.2 1.6 collective-permute-start.1
  18.7 1.2 slice_bitcast_fusion.3
  19.9 1.6 collective-permute-start.2
  22.0 1.5 collective-permute-start.8
  25.0 1.2 slice.247
  28.3 1.5 fusion.7
  31.0 1.2 subtract_convert_fusion
  32.2 1.2 select_convert_fusion.kx_ref
  33.4 2.3 pad_maximum_fusion
  36.2 1.6 collective-permute-start.3
  37.9 2.7 collective-permute-done.5
  40.6 2.2 collective-permute-done.3
  42.7 2.5 collective-permute-done.4
  48.2 5.6 %collective-permute-done.6 = bf16[2,2,48,768]{3,2,1,0:T(8,128)(2,1)S(1)} collective-permute-done((bf16[2,2,48,768]{3,2,1,0:T(8,128)(2,1)}, bf16[2,2,48,768]{3,2,1,0:T(8,128)(2,1)S(1)}, u32[]{:S(2)}, u32[]{:S(2)}) %collective-permute-start.6) | collective-permute-done | bytes 294944 | tf_op jit(solution)/shard_map/ppermute | solution.py:721
  56.3 2.9 maximum_select_fusion
  61.3 2.2 maximum_select_fusion.5
  63.8 1.1 copy-done.14
  65.1 1.2 maximum_select_fusion.6
  66.3 1.2 maximum_select_fusion.2
  67.5 4.3 %convolution_convert_fusion.rel_ref = bf16[2432,384]{1,0:T(8,128)(2,1)S(1)} fusion(bf16[2432,768]{1,0:T(8,128)(2,1)} %pad_maximum_fusion, bf16[768,896]{1,0:T(8,128)(2,1)S(1)} %bitcast.184), kind=kOutput, calls=%fused_computation | convolution fusion | flops 1435385856 | bytes 6193152 | tf_op jit(solution)/shard_map/dot_general | solution.py:39
  71.9 4.1 %convolution_convert_fusion.1.q_ref.k_ref.v_ref = bf16[1664,768]{1,0:T(8,128)(2,1)S(1)} fusion(bf16[768,768]{1,0:T(8,128)(2,1)} %bitcast.36, bf16[384,768]{1,0:T(8,128)(2,1)S(1)} %copy-done.19, bf16[256,768]{1,0:T(8,128)(2,1)S(1)} %maximum_select_fusion.6, bf16[1024,768]{1,0:T(8,128)(2,1)S(1)} %copy-done.17), kind=kOutput, calls=%fused_computation.4 | convolution fusion | flops 1971879936 | bytes 6291456 | tf_op jit(solution)/shard_map/dot_general | solution.py:39
  76.0 16.0 %shard_map.332 = (bf16[1280,128]{1,0:T(8,128)(2,1)S(1)}, bf16[5,2,256,1408]{3,2,1,0:T(8,128)(2,1)}, f32[1280,128]{1,0:T(8,128)S(1)}) custom-call(s32[4]{0:T(128)S(1)} %bitcast.176, bf16[1664,768]{1,0:T(8,128)(2,1)S(1)} %convolution_convert_fusion.1.q_ref.k_ref.v_ref, bf16[1664,768]{1,0:T(8,128)(2,1)S(1)} %convolution_convert_fusion.1.q_ref.k_ref.v_ref, ...), custom_call_target="tpu_custom_call" | custom-call | flops 29527900160 | bytes 7208960 | tf_op jit(solution)/shard_map/pallas_call | solution.py:351
  92.0 1.5 collective-permute-start.12
  93.6 16.2 %shard_map.333 = (bf16[1280,128]{1,0:T(8,128)(2,1)S(1)}, bf16[5,2,256,1408]{3,2,1,0:T(8,128)(2,1)}, f32[1280,128]{1,0:T(8,128)S(1)}) custom-call(s32[4]{0:T(128)S(1)} %bitcast.177, bf16[1664,768]{1,0:T(8,128)(2,1)S(1)} %convolution_convert_fusion.1.q_ref.k_ref.v_ref, bf16[1664,768]{1,0:T(8,128)(2,1)S(1)} %convolution_convert_fusion.1.q_ref.k_ref.v_ref, ...), custom_call_target="tpu_custom_call" | custom-call | flops 29527900160 | bytes 7208960 | tf_op jit(solution)/shard_map/pallas_call | solution.py:351
  110.7 1.5 convolution_convert_fusion.2.q_ref.k_ref.v_ref
  112.2 16.0 %shard_map.334 = (bf16[1280,128]{1,0:T(8,128)(2,1)S(1)}, bf16[5,2,256,1408]{3,2,1,0:T(8,128)(2,1)}, f32[1280,128]{1,0:T(8,128)S(1)}) custom-call(s32[4]{0:T(128)S(1)} %bitcast.178, bf16[1664,384]{1,0:T(8,128)(2,1)S(1)} %convolution_convert_fusion.2.q_ref.k_ref.v_ref, bf16[1664,384]{1,0:T(8,128)(2,1)S(1)} %convolution_convert_fusion.2.q_ref.k_ref.v_ref, ...), custom_call_target="tpu_custom_call" | custom-call | flops 29527900160 | bytes 7208960 | tf_op jit(solution)/shard_map/pallas_call | solution.py:351
  129.7 1.5 collective-permute-start.14
  131.2 4.2 %collective-permute-done.13 = bf16[640,128]{1,0:T(8,128)(2,1)S(1)} collective-permute-done((bf16[640,128]{1,0:T(8,128)(2,1)S(1)}, bf16[640,128]{1,0:T(8,128)(2,1)S(1)}, u32[]{:S(2)}, u32[]{:S(2)}) %collective-permute-start.13) | collective-permute-done | bytes 163872 | tf_op jit(solution)/shard_map/ppermute | solution.py:712
  135.4 2.2 collective-permute-done.14
  139.6 1.5 collective-permute-start.24
  141.1 1.4 all-gather.2.cloned.1.call-done.weights_ref
  145.9 38.6 %shard_map.335 = (bf16[640,768]{1,0:T(8,128)(2,1)}, f32[640,768]{1,0:T(8,128)}, bf16[768,6912]{1,0:T(8,128)(2,1)}, f32[1,3072]{1,0:T(1,128)}, f32[8,768]{1,0:T(8...) custom-call(s32[1]{0:T(128)} %bitcast.side_ref, ...), custom_call_target="tpu_custom_call" | custom-call | flops 18119393280 | bytes 47185920 | tf_op jit(solution)/shard_map/pallas_call | solution.py:666
  184.5 2.1 slice_bitcast_fusion.1
  186.6 1.6 slice_bitcast_fusion.5
  189.1 1.5 collective-permute-start.15
  192.0 1.5 collective-permute-start.19
  193.5 2.6 collective-permute-done.15.far_ref
  196.2 22.0 %shard_map.336 = (bf16[1664,384]{1,0:T(8,128)(2,1)S(1)}, bf16[2432,128]{1,0:T(8,128)(2,1)S(1)}, f32[8,128]{1,0:T(8,128)S(1)}) custom-call(s32[5]{0:T(128)S(1)} %pad_add_fusion.1.order_ref, bf16[1664,768]{1,0:T(8,128)(2,1)} %copy-done.3, bf16[1664,768]{1,0:T(8,128)(2,1)} %copy-done.3, bf16[1664,768]{1,0:T(8,128)(2,1)} %copy-done.3, ...), custom_call_target="tpu_custom_call" | custom-call | flops 44291850240 | bytes 7208960 | tf_op jit(solution)/shard_map/pallas_call | solution.py:383
  218.2 1.6 convolution_convert_fusion.5
  220.8 1.2 convolution_convert_fusion.9
  226.1 4.5 %all-to-all-start = ((bf16[8,56,512]{2,1,0:T(8,128)(2,1)}), bf16[8,56,512]{2,1,0:T(8,128)(2,1)}, u32[]{:S(2)}, u32[]{:S(2)}) async-start(bf16[8,56,512]{2,1,0:T(8,128)(2,1)} %add_convert_fusion.2), calls=%async_computation | async-start | bytes 917504 | tf_op jit(solution)/shard_map/all_to_all | solution.py:980
  231.7 21.3 %shard_map.337 = (bf16[1664,384]{1,0:T(8,128)(2,1)S(1)}, bf16[2432,128]{1,0:T(8,128)(2,1)S(1)}, f32[8,128]{1,0:T(8,128)S(1)}) custom-call(s32[5]{0:T(128)S(1)} %pad_add_fusion.1.order_ref, bf16[1664,768]{1,0:T(8,128)(2,1)} %copy-done.3, bf16[1664,768]{1,0:T(8,128)(2,1)} %copy-done.3, bf16[1664,768]{1,0:T(8,128)(2,1)} %copy-done.3, ...), custom_call_target="tpu_custom_call" | custom-call | flops 44291850240 | bytes 7208960 | tf_op jit(solution)/shard_map/pallas_call | solution.py:383
  253.0 5.2 %all-to-all-done = bf16[8,56,512]{2,1,0:T(8,128)(2,1)} async-done(((bf16[8,56,512]{2,1,0:T(8,128)(2,1)}), bf16[8,56,512]{2,1,0:T(8,128)(2,1)}, u32[]{:S(2)}, u32[]{:S(2)}) %all-to-all-start) | async-done | bytes 458784 | tf_op jit(solution)/shard_map/all_to_all | solution.py:980
  259.3 3.4 convolution_convert_fusion.4
  262.8 1.2 convolution_convert_fusion.8
  266.9 4.4 %all-to-all-start.1 = ((bf16[8,48,512]{2,1,0:T(8,128)(2,1)}), bf16[8,48,512]{2,1,0:T(8,128)(2,1)}, u32[]{:S(2)}, u32[]{:S(2)}) async-start(bf16[8,48,512]{2,1,0:T(8,128)(2,1)} %add_convert_fusion.3), calls=%async_computation.1 | async-start | bytes 786432 | tf_op jit(solution)/shard_map/all_to_all | solution.py:980
  271.3 1.1 copy-done.7
  272.4 21.3 %shard_map.338 = (bf16[1664,384]{1,0:T(8,128)(2,1)S(1)}, bf16[2432,128]{1,0:T(8,128)(2,1)S(1)}, f32[8,128]{1,0:T(8,128)S(1)}) custom-call(s32[5]{0:T(128)S(1)} %pad_add_fusion.1.order_ref, bf16[1664,384]{1,0:T(8,128)(2,1)} %copy-done.2, bf16[1664,384]{1,0:T(8,128)(2,1)} %copy-done.2, bf16[1664,384]{1,0:T(8,128)(2,1)} %copy-done.2, ...), custom_call_target="tpu_custom_call" | custom-call | flops 44291850240 | bytes 7208960 | tf_op jit(solution)/shard_map/pallas_call | solution.py:383
  295.8 3.3 convolution_convert_fusion.3
  299.3 1.9 copy-done.13
  301.2 1.2 convolution_convert_fusion.7
  302.9 1.2 copy-done.32
  304.2 1.9 collective-permute-start.23
  307.1 1.1 constant_dynamic-update-slice_fusion.23
  308.3 5.4 %fusion = f32[640,768]{1,0:T(8,128)} fusion(bf16[640,1920]{1,0:T(8,128)(2,1)S(1)} %constant_dynamic-update-slice_fusion.23, bf16[768,768]{1,0:T(8,128)(2,1)} %collective-permute-done.22, bf16[768,384]{1,0:T(8,128)(2,1)} %slice.314, bf16[768,768]{1,0:T(8,128)(2,1)} %bitcast.36), kind=kOutput, calls=%fused_computation.5 | convolution fusion | flops 1896284160 | bytes 7372800 | tf_op jit(solution)/shard_map/dot_general | solution.py:43
  314.6 5.8 %all-to-all-start.2 = ((bf16[8,56,512]{2,1,0:T(8,128)(2,1)}), bf16[8,56,512]{2,1,0:T(8,128)(2,1)S(1)}, u32[]{:S(2)}, u32[]{:S(2)}) async-start(bf16[8,56,512]{2,1,0:T(8,128)(2,1)} %add_convert_fusion.1), calls=%async_computation.2 | async-start | bytes 917504 | tf_op jit(solution)/shard_map/all_to_all | solution.py:980
  320.4 3.0 add_add_fusion
  323.5 1.2 slice_bitcast_fusion
  324.8 1.1 constant_dynamic-slice_fusion.4
  325.9 1.5 collective-permute-start.26
  328.2 5.3 %all-to-all-done.2 = bf16[8,56,512]{2,1,0:T(8,128)(2,1)S(1)} async-done(((bf16[8,56,512]{2,1,0:T(8,128)(2,1)}), bf16[8,56,512]{2,1,0:T(8,128)(2,1)S(1)}, u32[]{:S(2)}, u32[]{:S(2)}) %all-to-all-start.2) | async-done | bytes 458784 | tf_op jit(solution)/shard_map/all_to_all | solution.py:980
  333.6 1.5 collective-permute-done.26
  336.5 1.1 collective-permute-start.28
  (325 shorter events, 56.8 us)
Async XLA Ops:
  7.2 135.3 %all-gather.2.cloned.1.call-start = ((), (), s32[]{:S(2)}) async-start(), calls=%async_computation.4 | async-start | bytes 11489280 | tf_op jit(solution)/shard_map/all_gather | solution.py:869
  11.6 24.1 %collective-permute-start = (bf16[48,768]{1,0:T(8,128)(2,1)S(1)}, bf16[48,768]{1,0:T(8,128)(2,1)S(1)}, u32[]{:S(2)}, u32[]{:S(2)}) collective-permute-start(bf16[48,768]{1,0:T(8,128)(2,1)S(1)} %constant_dynamic-update-slice_fusion), channel_id=1, source_target_pairs={{0,8},{1,9},{2,10},{3,11},{4,12},{5,13},{6,14},{7,15},{8,0},{9,1},... | collective-permute-start | bytes 221192 | tf_op jit(solution)/shard_map/ppermute | solution.py:721
  17.1 13.4 %copy-start.26 = (bf16[192,768]{1,0:T(8,128)(2,1)S(1)}, bf16[192,768]{1,0:T(8,128)(2,1)}, u32[]{:S(2)}) copy-start(bf16[192,768]{1,0:T(8,128)(2,1)} %param.36) | copy-start | bytes 884740
  17.1 13.6 %copy-start.39 = (bf16[2,48]{1,0:T(2,128)(2,1)S(1)}, bf16[2,48]{1,0:T(2,128)(2,1)}, u32[]{:S(2)}) copy-start(bf16[2,48]{1,0:T(2,128)(2,1)} %param.38) | copy-start | bytes 580
  17.1 13.7 %copy-start.40 = (bf16[2,48]{1,0:T(2,128)(2,1)S(1)}, bf16[2,48]{1,0:T(2,128)(2,1)}, u32[]{:S(2)}) copy-start(bf16[2,48]{1,0:T(2,128)(2,1)} %param.39) | copy-start | bytes 580
  17.2 13.8 %slice-start.1 = ((s32[1,1408]{1,0:T(1,128)}), s32[1,1024]{1,0:T(1,128)S(1)}, s32[]{:S(2)}) async-start(s32[1,1408]{1,0:T(1,128)} %param.24), calls=%async_computation.7 | async-start | bytes 8192 | tf_op jit(solution)/shard_map/slice | solution.py:826
  17.2 18.6 %collective-permute-start.1 = (bf16[48,896]{1,0:T(8,128)(2,1)S(1)}, bf16[48,896]{1,0:T(8,128)(2,1)S(1)}, u32[]{:S(2)}, u32[]{:S(2)}) collective-permute-start(bf16[48,896]{1,0:T(8,128)(2,1)S(1)} %constant_dynamic-update-slice_fusion.6), channel_id=1, source_target_pairs={{0,2},{1,3},{2,0},{3,1},{4,6},{5,7},{6,4},{7,5},{8,10},{9,11},{10,... | collective-permute-start | bytes 258056 | tf_op jit(solution)/shard_map/ppermute | solution.py:721
  19.9 15.8 %collective-permute-start.2 = (bf16[256,768]{1,0:T(8,128)(2,1)S(1)}, bf16[256,768]{1,0:T(8,128)(2,1)S(1)}, u32[]{:S(2)}, u32[]{:S(2)}) collective-permute-start(bf16[256,768]{1,0:T(8,128)(2,1)S(1)} %get-tuple-element.154), channel_id=1, source_target_pairs={{0,16},{16,0},{1,17},{17,1},{2,18},{18,2},{3,19},{19,3},{4,20},{20... | collective-permute-start | bytes 1179656 | tf_op jit(solution)/shard_map/ppermute | solution.py:712
  21.5 19.1 %collective-permute-start.5 = (bf16[256,768]{1,0:T(8,128)(2,1)S(1)}, bf16[256,768]{1,0:T(8,128)(2,1)}, u32[]{:S(2)}, u32[]{:S(2)}) collective-permute-start(bf16[256,768]{1,0:T(8,128)(2,1)S(1)} %get-tuple-element.153), channel_id=1, source_target_pairs={{0,16},{16,0},{1,17},{17,1},{2,18},{18,2},{3,19},{19,3},{4,20},{20... | collective-permute-start | bytes 1179656 | tf_op jit(solution)/shard_map/ppermute | solution.py:712
  22.0 26.2 %collective-permute-start.8 = (bf16[192,768]{1,0:T(8,128)(2,1)}, bf16[192,768]{1,0:T(8,128)(2,1)}, u32[]{:S(2)}, u32[]{:S(2)}) collective-permute-start(bf16[192,768]{1,0:T(8,128)(2,1)} %bitcast.229), channel_id=1, source_target_pairs={{0,16},{16,0},{1,17},{17,1},{2,18},{18,2},{3,19},{19,3},{4,20},{20... | collective-permute-start | bytes 884744 | tf_op jit(solution)/shard_map/ppermute | solution.py:712
  35.6 11.6 %copy-start.33 = (bf16[48,768]{1,0:T(8,128)(2,1)S(1)}, bf16[48,768]{1,0:T(8,128)(2,1)}, u32[]{:S(2)}) copy-start(bf16[48,768]{1,0:T(8,128)(2,1)} %param.30) | copy-start | bytes 221188
  35.6 19.4 %copy-start = (s32[1,4]{1,0:T(1,128)S(1)}, s32[1,4]{1,0:T(1,128)}, u32[]{:S(2)}) copy-start(s32[1,4]{1,0:T(1,128)} %param.25) | copy-start | bytes 52
  35.7 11.5 %copy-start.24 = (bf16[256,768]{1,0:T(8,128)(2,1)}, bf16[256,768]{1,0:T(8,128)(2,1)S(1)}, u32[]{:S(2)}) copy-start(bf16[256,768]{1,0:T(8,128)(2,1)S(1)} %collective-permute-done.2) | copy-start | bytes 1179652
  35.8 9.4 %collective-permute-start.4 = (bf16[2,48,896]{2,1,0:T(8,128)(2,1)S(1)}, bf16[2,48,896]{2,1,0:T(8,128)(2,1)S(1)}, u32[]{:S(2)}, u32[]{:S(2)}) collective-permute-start(bf16[2,48,896]{2,1,0:T(8,128)(2,1)S(1)} %maximum_select_fusion.10), channel_id=1, source_target_pairs={{0,8},{1,9},{2,10},{3,11},{4,12},{5,13},{6,14},{7,15},{8,0},{9,1},... | collective-permute-start | bytes 516104 | tf_op jit(solution)/shard_map/ppermute | solution.py:721
  36.2 6.5 %collective-permute-start.3 = (bf16[2,48,768]{2,1,0:T(8,128)(2,1)S(1)}, bf16[2,48,768]{2,1,0:T(8,128)(2,1)S(1)}, u32[]{:S(2)}, u32[]{:S(2)}) collective-permute-start(bf16[2,48,768]{2,1,0:T(8,128)(2,1)S(1)} %maximum_select_fusion.12), channel_id=1, source_target_pairs={{0,4},{1,5},{2,6},{3,7},{4,0},{5,1},{6,2},{7,3},{8,12},{9,13},{10,... | collective-permute-start | bytes 442376 | tf_op jit(solution)/shard_map/ppermute | solution.py:721
  46.0 8.1 %collective-permute-start.7 = (bf16[2,2,48,896]{3,2,1,0:T(8,128)(2,1)}, bf16[2,2,48,896]{3,2,1,0:T(8,128)(2,1)S(1)}, u32[]{:S(2)}, u32[]{:S(2)}) collective-permute-start(bf16[2,2,48,896]{3,2,1,0:T(8,128)(2,1)} %maximum_select_fusion.7), channel_id=1, source_target_pairs={{0,4},{1,5},{2,6},{3,7},{4,0},{5,1},{6,2},{7,3},{8,12},{9,13},{10,... | collective-permute-start | bytes 1032200 | tf_op jit(solution)/shard_map/ppermute | solution.py:721
  46.7 7.1 %collective-permute-start.6 = (bf16[2,2,48,768]{3,2,1,0:T(8,128)(2,1)}, bf16[2,2,48,768]{3,2,1,0:T(8,128)(2,1)S(1)}, u32[]{:S(2)}, u32[]{:S(2)}) collective-permute-start(bf16[2,2,48,768]{3,2,1,0:T(8,128)(2,1)} %maximum_select_fusion.9), channel_id=1, source_target_pairs={{0,2},{1,3},{2,0},{3,1},{4,6},{5,7},{6,4},{7,5},{8,10},{9,11},{10,... | collective-permute-start | bytes 884744 | tf_op jit(solution)/shard_map/ppermute | solution.py:721
  48.2 8.1 %copy-start.16 = (bf16[1,512,768]{2,1,0:T(8,128)(2,1)S(1)}, bf16[1,512,768]{2,1,0:T(8,128)(2,1)}, u32[]{:S(2)}) copy-start(bf16[1,512,768]{2,1,0:T(8,128)(2,1)} %param.21) | copy-start | bytes 2359300
  54.1 270.6 %reduce-scatter.2.cloned.1.call-start = ((), (), s32[]{:S(2)}) async-start(), calls=%async_computation.5 | async-start | bytes 11280384 | tf_op jit(solution)/shard_map/reduce_scatter | solution.py:937
  54.4 9.2 %collective-permute-start.11 = (bf16[128,768]{1,0:T(8,128)(2,1)}, bf16[128,768]{1,0:T(8,128)(2,1)}, u32[]{:S(2)}, u32[]{:S(2)}) collective-permute-start(bf16[128,768]{1,0:T(8,128)(2,1)} %bitcast.235), channel_id=1, source_target_pairs={{0,16},{16,0},{1,17},{17,1},{2,18},{18,2},{3,19},{19,3},{4,20},{20... | collective-permute-start | bytes 589832 | tf_op jit(solution)/shard_map/ppermute | solution.py:712
  59.4 4.2 %collective-permute-start.10 = (bf16[2,2,2,48,896]{4,3,2,1,0:T(8,128)(2,1)S(1)}, bf16[2,2,2,48,896]{4,3,2,1,0:T(8,128)(2,1)S(1)}, u32[]{:S(2)}, u32[]{:S(2)}) collective-permute-start(bf16[2,2,2,48,896]{4,3,2,1,0:T(8,128)(2,1)S(1)} %maximum_select_fusion.3), channel_id=1, source_target_pairs={{0,1},{1,0},{2,3},{3,2},{4,5},{5,4},{6,7},{7,6},{8,9},{9,8},{10,11... | collective-permute-start | bytes 2064392 | tf_op jit(solution)/shard_map/ppermute | solution.py:721
  59.6 3.9 %collective-permute-start.9 = (bf16[2,2,2,48,768]{4,3,2,1,0:T(8,128)(2,1)S(1)}, bf16[2,2,2,48,768]{4,3,2,1,0:T(8,128)(2,1)S(1)}, u32[]{:S(2)}, u32[]{:S(2)}) collective-permute-start(bf16[2,2,2,48,768]{4,3,2,1,0:T(8,128)(2,1)S(1)} %maximum_select_fusion.4), channel_id=1, source_target_pairs={{0,1},{1,0},{2,3},{3,2},{4,5},{5,4},{6,7},{7,6},{8,9},{9,8},{10,11... | collective-permute-start | bytes 1769480 | tf_op jit(solution)/shard_map/ppermute | solution.py:721
  61.3 3.8 %copy-start.31 = (bf16[1,128,768]{2,1,0:T(8,128)(2,1)S(1)}, bf16[1,128,768]{2,1,0:T(8,128)(2,1)}, u32[]{:S(2)}) copy-start(bf16[1,128,768]{2,1,0:T(8,128)(2,1)} %param.22) | copy-start | bytes 589828
  65.1 2.4 copy-start.15
  66.3 44.3 %copy-start.21 = (bf16[256,768]{1,0:T(8,128)(2,1)}, bf16[256,768]{1,0:T(8,128)(2,1)S(1)}, u32[]{:S(2)}) copy-start(bf16[256,768]{1,0:T(8,128)(2,1)S(1)} %maximum_select_fusion.6) | copy-start | bytes 1179652
  67.5 4.4 %copy-start.17 = (bf16[1024,768]{1,0:T(8,128)(2,1)S(1)}, bf16[1024,768]{1,0:T(8,128)(2,1)}, u32[]{:S(2)}) copy-start(bf16[1024,768]{1,0:T(8,128)(2,1)} %maximum_select_fusion) | copy-start | bytes 4718596
  67.5 4.4 %copy-start.19 = (bf16[384,768]{1,0:T(8,128)(2,1)S(1)}, bf16[384,768]{1,0:T(8,128)(2,1)}, u32[]{:S(2)}) copy-start(bf16[384,768]{1,0:T(8,128)(2,1)} %maximum_select_fusion.5) | copy-start | bytes 1769476
  71.8 40.3 %copy-start.1 = (bf16[2432,384]{1,0:T(8,128)(2,1)}, bf16[2432,384]{1,0:T(8,128)(2,1)S(1)}, u32[]{:S(2)}) copy-start(bf16[2432,384]{1,0:T(8,128)(2,1)S(1)} %convolution_convert_fusion.rel_ref) | copy-start | bytes 5603332
  76.0 17.6 %copy-start.3 = (bf16[1664,768]{1,0:T(8,128)(2,1)}, bf16[1664,768]{1,0:T(8,128)(2,1)S(1)}, u32[]{:S(2)}) copy-start(bf16[1664,768]{1,0:T(8,128)(2,1)S(1)} %convolution_convert_fusion.1.q_ref.k_ref.v_ref) | copy-start | bytes 7667716
  92.0 39.1 %collective-permute-start.12 = (bf16[640,128]{1,0:T(8,128)(2,1)S(1)}, bf16[640,128]{1,0:T(8,128)(2,1)S(1)}, u32[]{:S(2)}, u32[]{:S(2)}) collective-permute-start(bf16[640,128]{1,0:T(8,128)(2,1)S(1)} %pad_maximum_fusion.19), channel_id=1, source_target_pairs={{0,16},{16,0},{1,17},{17,1},{2,18},{18,2},{3,19},{19,3},{4,20},{20... | collective-permute-start | bytes 491528 | tf_op jit(solution)/shard_map/ppermute | solution.py:712
  112.2 16.0 %copy-start.2 = (bf16[1664,384]{1,0:T(8,128)(2,1)}, bf16[1664,384]{1,0:T(8,128)(2,1)S(1)}, u32[]{:S(2)}) copy-start(bf16[1664,384]{1,0:T(8,128)(2,1)S(1)} %convolution_convert_fusion.2.q_ref.k_ref.v_ref) | copy-start | bytes 3833860
  128.2 9.8 %copy-start.6 = (f32[1280,128]{1,0:T(8,128)}, f32[1280,128]{1,0:T(8,128)S(1)}, u32[]{:S(2)}) copy-start(f32[1280,128]{1,0:T(8,128)S(1)} %get-tuple-element.121.inv_ref) | copy-start | bytes 1966084
  128.2 7.2 %collective-permute-start.13 = (bf16[640,128]{1,0:T(8,128)(2,1)S(1)}, bf16[640,128]{1,0:T(8,128)(2,1)S(1)}, u32[]{:S(2)}, u32[]{:S(2)}) collective-permute-start(bf16[640,128]{1,0:T(8,128)(2,1)S(1)} %pad_maximum_fusion.20), channel_id=1, source_target_pairs={{0,16},{16,0},{1,17},{17,1},{2,18},{18,2},{3,19},{19,3},{4,20},{20... | collective-permute-start | bytes 491528 | tf_op jit(solution)/shard_map/ppermute | solution.py:712
  129.7 7.9 %collective-permute-start.14 = (bf16[640,128]{1,0:T(8,128)(2,1)S(1)}, bf16[640,128]{1,0:T(8,128)(2,1)S(1)}, u32[]{:S(2)}, u32[]{:S(2)}) collective-permute-start(bf16[640,128]{1,0:T(8,128)(2,1)S(1)} %pad_maximum_fusion.21), channel_id=1, source_target_pairs={{0,16},{16,0},{1,17},{17,1},{2,18},{18,2},{3,19},{19,3},{4,20},{20... | collective-permute-start | bytes 491528 | tf_op jit(solution)/shard_map/ppermute | solution.py:712
  139.1 169.2 %collective-permute-start.22 = (bf16[768,768]{1,0:T(8,128)(2,1)}, bf16[768,768]{1,0:T(8,128)(2,1)}, u32[]{:S(2)}, u32[]{:S(2)}) collective-permute-start(bf16[768,768]{1,0:T(8,128)(2,1)} %bitcast.36), channel_id=1, source_target_pairs={{0,16},{16,0},{1,17},{17,1},{2,18},{18,2},{3,19},{19,3},{4,20},{20... | collective-permute-start | bytes 3538952 | tf_op jit(solution)/shard_map/ppermute | solution.py:712
  139.6 180.8 %collective-permute-start.24 = (bf16[768,384]{1,0:T(8,128)(2,1)}, bf16[768,384]{1,0:T(8,128)(2,1)}, u32[]{:S(2)}, u32[]{:S(2)}) collective-permute-start(bf16[768,384]{1,0:T(8,128)(2,1)} %slice.314), channel_id=1, source_target_pairs={{0,16},{16,0},{1,17},{17,1},{2,18},{18,2},{3,19},{19,3},{4,20},{20... | collective-permute-start | bytes 1769480 | tf_op jit(solution)/shard_map/ppermute | solution.py:712
  188.2 2.8 copy-start.35
  188.2 7.9 %copy-start.10 = (bf16[640,128]{1,0:T(8,128)(2,1)S(1)}, bf16[640,128]{1,0:T(8,128)(2,1)}, u32[]{:S(2)}) copy-start(bf16[640,128]{1,0:T(8,128)(2,1)} %get-tuple-element.99.near_ref) | copy-start | bytes 491524
  189.1 7.0 %collective-permute-start.15 = (bf16[640,128]{1,0:T(8,128)(2,1)S(1)}, bf16[640,128]{1,0:T(8,128)(2,1)S(1)}, u32[]{:S(2)}, u32[]{:S(2)}) collective-permute-start(bf16[640,128]{1,0:T(8,128)(2,1)S(1)} %copy-done.38), channel_id=1, source_target_pairs={{0,16},{16,0},{1,17},{17,1},{2,18},{18,2},{3,19},{19,3},{4,20},{20... | collective-permute-start | bytes 491528 | tf_op jit(solution)/shard_map/ppermute | solution.py:712
  191.4 39.2 %collective-permute-start.17 = (bf16[640,128]{1,0:T(8,128)(2,1)}, bf16[640,128]{1,0:T(8,128)(2,1)S(1)}, u32[]{:S(2)}, u32[]{:S(2)}) collective-permute-start(bf16[640,128]{1,0:T(8,128)(2,1)} %get-tuple-element.109), channel_id=1, source_target_pairs={{0,16},{16,0},{1,17},{17,1},{2,18},{18,2},{3,19},{19,3},{4,20},{20... | collective-permute-start | bytes 491528 | tf_op jit(solution)/shard_map/ppermute | solution.py:712
  192.0 79.3 %collective-permute-start.19 = (bf16[640,128]{1,0:T(8,128)(2,1)}, bf16[640,128]{1,0:T(8,128)(2,1)S(1)}, u32[]{:S(2)}, u32[]{:S(2)}) collective-permute-start(bf16[640,128]{1,0:T(8,128)(2,1)} %get-tuple-element.120), channel_id=1, source_target_pairs={{0,16},{16,0},{1,17},{17,1},{2,18},{18,2},{3,19},{19,3},{4,20},{20... | collective-permute-start | bytes 491528 | tf_op jit(solution)/shard_map/ppermute | solution.py:712
  196.1 22.1 %copy-start.18 = (bf16[1024,768]{1,0:T(8,128)(2,1)S(1)}, bf16[1024,768]{1,0:T(8,128)(2,1)}, u32[]{:S(2)}) copy-start(bf16[1024,768]{1,0:T(8,128)(2,1)} %maximum_select_fusion) | copy-start | bytes 4718596
  196.1 22.1 %copy-start.20 = (bf16[384,768]{1,0:T(8,128)(2,1)S(1)}, bf16[384,768]{1,0:T(8,128)(2,1)}, u32[]{:S(2)}) copy-start(bf16[384,768]{1,0:T(8,128)(2,1)} %maximum_select_fusion.5) | copy-start | bytes 1769476
  196.1 22.1 %copy-start.22 = (bf16[256,768]{1,0:T(8,128)(2,1)S(1)}, bf16[256,768]{1,0:T(8,128)(2,1)}, u32[]{:S(2)}) copy-start(bf16[256,768]{1,0:T(8,128)(2,1)} %copy-done.21) | copy-start | bytes 1179652
  218.2 2.6 copy-start.11
  222.2 1.9 collective-permute-start.16
  222.4 8.2 %copy-start.9 = (bf16[640,128]{1,0:T(8,128)(2,1)S(1)}, bf16[640,128]{1,0:T(8,128)(2,1)}, u32[]{:S(2)}) copy-start(bf16[640,128]{1,0:T(8,128)(2,1)} %get-tuple-element.108.near_ref) | copy-start | bytes 491524
  224.1 80.1 %collective-permute-start.20 = (bf16[640,384]{1,0:T(8,128)(2,1)}, bf16[640,384]{1,0:T(8,128)(2,1)}, u32[]{:S(2)}, u32[]{:S(2)}) collective-permute-start(bf16[640,384]{1,0:T(8,128)(2,1)} %pad_maximum_fusion.10), channel_id=1, source_target_pairs={{0,16},{16,0},{1,17},{17,1},{2,18},{18,2},{3,19},{19,3},{4,20},{20... | collective-permute-start | bytes 1474568 | tf_op jit(solution)/shard_map/ppermute | solution.py:712
  226.1 32.1 %all-to-all-start = ((bf16[8,56,512]{2,1,0:T(8,128)(2,1)}), bf16[8,56,512]{2,1,0:T(8,128)(2,1)}, u32[]{:S(2)}, u32[]{:S(2)}) async-start(bf16[8,56,512]{2,1,0:T(8,128)(2,1)} %add_convert_fusion.2), calls=%async_computation | async-start | bytes 917504 | tf_op jit(solution)/shard_map/all_to_all | solution.py:980
  259.3 3.5 copy-start.12
  264.1 1.9 collective-permute-start.18
  264.3 7.0 %copy-start.8 = (bf16[640,128]{1,0:T(8,128)(2,1)S(1)}, bf16[640,128]{1,0:T(8,128)(2,1)}, u32[]{:S(2)}) copy-start(bf16[640,128]{1,0:T(8,128)(2,1)} %get-tuple-element.119.near_ref) | copy-start | bytes 491524
  266.1 41.1 %collective-permute-start.21 = (bf16[640,384]{1,0:T(8,128)(2,1)}, bf16[640,384]{1,0:T(8,128)(2,1)}, u32[]{:S(2)}, u32[]{:S(2)}) collective-permute-start(bf16[640,384]{1,0:T(8,128)(2,1)} %pad_maximum_fusion.11), channel_id=1, source_target_pairs={{0,16},{16,0},{1,17},{17,1},{2,18},{18,2},{3,19},{19,3},{4,20},{20... | collective-permute-start | bytes 1474568 | tf_op jit(solution)/shard_map/ppermute | solution.py:712
  266.9 27.7 %all-to-all-start.1 = ((bf16[8,48,512]{2,1,0:T(8,128)(2,1)}), bf16[8,48,512]{2,1,0:T(8,128)(2,1)}, u32[]{:S(2)}, u32[]{:S(2)}) async-start(bf16[8,48,512]{2,1,0:T(8,128)(2,1)} %add_convert_fusion.3), calls=%async_computation.1 | async-start | bytes 786432 | tf_op jit(solution)/shard_map/all_to_all | solution.py:980
  295.7 40.4 %copy-start.23 = (f32[48,512]{1,0:T(8,128)}, f32[48,512]{1,0:T(8,128)S(1)}, u32[]{:S(2)}) copy-start(f32[48,512]{1,0:T(8,128)S(1)} %convert_reduce_fusion.3) | copy-start | bytes 294916
  302.5 11.2 %collective-permute-start.25 = (bf16[8,56,512]{2,1,0:T(8,128)(2,1)S(1)}, bf16[8,56,512]{2,1,0:T(8,128)(2,1)S(1)}, u32[]{:S(2)}, u32[]{:S(2)}) collective-permute-start(bf16[8,56,512]{2,1,0:T(8,128)(2,1)S(1)} %pad_maximum_fusion.14), channel_id=1, source_target_pairs={{0,1},{1,0},{2,3},{3,2},{4,5},{5,4},{6,7},{7,6},{8,9},{9,8},{10,11... | collective-permute-start | bytes 1376264 | tf_op jit(solution)/shard_map/ppermute | solution.py:721
  304.2 16.3 %collective-permute-start.23 = (bf16[640,384]{1,0:T(8,128)(2,1)S(1)}, bf16[640,384]{1,0:T(8,128)(2,1)S(1)}, u32[]{:S(2)}, u32[]{:S(2)}) collective-permute-start(bf16[640,384]{1,0:T(8,128)(2,1)S(1)} %pad_maximum_fusion.12), channel_id=1, source_target_pairs={{0,16},{16,0},{1,17},{17,1},{2,18},{18,2},{3,19},{19,3},{4,20},{20... | collective-permute-start | bytes 1474568 | tf_op jit(solution)/shard_map/ppermute | solution.py:712
  308.3 5.4 %copy-start.30 = (bf16[8,8,512]{2,1,0:T(8,128)(2,1)S(1)}, bf16[8,8,512]{2,1,0:T(8,128)(2,1)}, u32[]{:S(2)}) copy-start(bf16[8,8,512]{2,1,0:T(8,128)(2,1)} %get-tuple-element.214) | copy-start | bytes 196612
  314.6 18.9 %all-to-all-start.2 = ((bf16[8,56,512]{2,1,0:T(8,128)(2,1)}), bf16[8,56,512]{2,1,0:T(8,128)(2,1)S(1)}, u32[]{:S(2)}, u32[]{:S(2)}) async-start(bf16[8,56,512]{2,1,0:T(8,128)(2,1)} %add_convert_fusion.1), calls=%async_computation.2 | async-start | bytes 917504 | tf_op jit(solution)/shard_map/all_to_all | solution.py:980
  325.9 9.2 %collective-permute-start.26 = (bf16[1,24,6912]{2,1,0:T(8,128)(2,1)S(1)}, bf16[1,24,6912]{2,1,0:T(8,128)(2,1)}, u32[]{:S(2)}, u32[]{:S(2)}) collective-permute-start(bf16[1,24,6912]{2,1,0:T(8,128)(2,1)S(1)} %get-tuple-element.158), channel_id=1, source_target_pairs={{0,16},{16,0},{1,17},{17,1},{2,18},{18,2},{3,19},{19,3},{4,20},{20... | collective-permute-start | bytes 995336 | tf_op jit(solution)/shard_map/ppermute | solution.py:712
  336.2 3.3 copy-start.29
  336.4 3.5 slice-start
  336.5 7.5 %collective-permute-start.28 = (bf16[512]{0:T(512)(128)(2,1)S(1)}, bf16[512]{0:T(512)(128)(2,1)S(1)}, u32[]{:S(2)}, u32[]{:S(2)}) collective-permute-start(bf16[512]{0:T(512)(128)(2,1)S(1)} %fusion.35), channel_id=1, source_target_pairs={{0,16},{16,0},{1,17},{17,1},{2,18},{18,2},{3,19},{19,3},{4,20},{20... | collective-permute-start | bytes 3080 | tf_op jit(solution)/shard_map/ppermute | solution.py:712
  337.7 8.7 %collective-permute-start.27 = (bf16[24,1152]{1,0:T(8,128)(2,1)S(1)}, bf16[24,1152]{1,0:T(8,128)(2,1)S(1)}, u32[]{:S(2)}, u32[]{:S(2)}) collective-permute-start(bf16[24,1152]{1,0:T(8,128)(2,1)S(1)} %dynamic-slice_convert_fusion), channel_id=1, source_target_pairs={{0,16},{16,0},{1,17},{17,1},{2,18},{18,2},{3,19},{19,3},{4,20},{20... | collective-permute-start | bytes 165896 | tf_op jit(solution)/shard_map/ppermute | solution.py:712
  (13 other events, 19.4 us)
Sparse Core Ops, SparseCore 0:
  54.3 88.2 all-gather.1
  188.4 135.6 reduce-scatter.1

commit v2 on v1

--- a/solution.py
+++ b/solution.py
@@ -348,6 +348,7 @@
 
 def attention_forward(pair, first, order, qkv, rel, marks, par):
     ins, exps = attention_specs(pair, first)
+    qkv, rel = (pltpu.with_memory_space_constraint(t, pltpu.HBM) for t in (qkv, rel))
     return pl.pallas_call(
         forward_kernel,
         grid_spec=pltpu.PrefetchScalarGridSpec(
@@ -943,15 +944,6 @@
         token_sums = lax.psum_scatter(
             grad_weights, ("seq", "fsdp"), scatter_dimension=0, tiled=True
         )[None]
-    grad_b_inner = grad_b_inner.reshape(blocks, width).T.reshape(devices, -1)
-    row_count = width // devices
-    token_flat = jnp.concatenate(
-        [
-            grad_b_inner.reshape(devices, -1),
-            grad_small[:5].reshape(5, devices, -1).transpose(1, 0, 2).reshape(devices, -1),
-        ],
-        1,
-    )
     inner_count = ffn_width // devices
 
     weights_two = weights_two[:, :pair_width]
@@ -1006,6 +998,18 @@
             inner_cols(pos_table, drel).astype(BF).reshape(groups, shard_rows, LANES),
         ]
         if pair == 0:
+            drel, grad_b_inner, grad_small = lax.optimization_barrier(
+                (drel, grad_b_inner, grad_small)
+            )
+            grad_b_inner = grad_b_inner.reshape(blocks, width).T.reshape(devices, -1)
+            row_count = width // devices
+            token_flat = jnp.concatenate(
+                [
+                    grad_b_inner.reshape(devices, -1),
+                    grad_small[:5].reshape(5, devices, -1).transpose(1, 0, 2).reshape(devices, -1),
+                ],
+                1,
+            )
             token_flat = token_flat.reshape(2, groups, -1).transpose(1, 0, 2).astype(BF)
             extra = ((0, 0), (0, 6), (0, pair_width + LANES - token_flat.shape[2]))
             parts.append(jnp.pad(token_flat, extra))

time: 362 us -> 367 us (1.014)
  matrix products: 32.1 us -> 37.5 us
  Pallas kernels: 151 us -> 155 us
    unnamed x107 -> x103, local copies, waits for them, and re-layouts: 16.3 us -> 18.1 us
  transfers between devices with their start and end apart: 34 -> 34, of which waited for: 12 -> 11; matrix products, arithmetic and copies ran while one was open for 25% -> 26% of each run, Pallas kernels for 43% -> 43%
where the time goes in v2:
time: 367 us; the launch traced here: 361 us
  Pallas kernels  155 us (42%)
  local copies, waits for them, and re-layouts  42.9 us (12%)
  starting transfers between devices  42.2 us (11%)
  matrix products  37.5 us (10%)
  waiting for transfers between devices  34.1 us (9%)
  other arithmetic  32.7 us (9%)
  between operations  16.6 us (5%)
    pallas_call x3, Pallas kernels, attention_backward(): pl.pallas_call(backward_kernel, grid_spec=pltpu.PrefetchScalarGridSpec(nu...  64.9 us
    pallas_call x3, Pallas kernels, attention_forward(): pl.pallas_call(forward_kernel, grid_spec=pltpu.PrefetchScalarGridSpec(num...  51.6 us
    pallas_call x1, Pallas kernels, middle(): pl.pallas_call(functools.partial(middle_kernel, groups), grid_spec=pltpu....  38.4 us
    ppermute x18, starting transfers between devices, swap(): return lax.ppermute(values, 'seq', [(0, 1), (1, 0)])  18.6 us
    unnamed x103, local copies, waits for them, and re-layouts  18.1 us
    dot_general x6, matrix products, inner_cols(): lax.dot_general(left, right, (((0,), (0,)), ((), ())), preferred_element_...  14.2 us
    all_to_all x3, starting transfers between devices, sum_message(): lax.all_to_all(message, 'fsdp', split_axis=0, concat_axis=0, tiled=True,...  14.1 us
    dot_general x4, matrix products, product(): return jnp.dot(left, right, preferred_element_type=F32)  13.5 us
  transfers between devices with their start and end apart: 34, of which 11 were waited for; matrix products, arithmetic and copies ran while one was open for 26% of the time, Pallas kernels for 43%

profile of v2, /device:TPU:0, one launch (start us, length us, event | category | flops | bytes accessed | tf_op | source)
XLA Modules:
  0.0 360.9 jit_solution(4711892301120136746)
XLA Ops:
  11.6 4.0 %collective-permute-start = (bf16[48,768]{1,0:T(8,128)(2,1)S(1)}, bf16[48,768]{1,0:T(8,128)(2,1)S(1)}, u32[]{:S(2)}, u32[]{:S(2)}) collective-permute-start(bf16[48,768]{1,0:T(8,128)(2,1)S(1)} %constant_dynamic-update-slice_fusion), channel_id=1, source_target_pairs={{0,8},{1,9},{2,10},{3,11},{4,12},{5,13},{6,14},{7,15},{8,0},{9,1},... | collective-permute-start | bytes 221192 | tf_op jit(solution)/shard_map/ppermute | solution.py:722
  17.2 1.6 collective-permute-start.1
  18.7 1.2 slice_bitcast_fusion.3
  19.9 1.6 collective-permute-start.2
  22.0 1.5 collective-permute-start.8
  25.0 1.2 slice.247
  28.3 1.5 fusion.7
  30.5 1.1 reshape.1020
  31.9 1.2 subtract_convert_fusion
  33.1 1.2 select_convert_fusion.kx_ref
  34.3 2.3 pad_maximum_fusion
  37.1 1.6 collective-permute-start.3
  38.8 1.7 collective-permute-done.5
  40.5 3.1 collective-permute-done.3
  43.7 2.4 collective-permute-done.4
  48.4 5.7 %collective-permute-done.6 = bf16[2,2,48,768]{3,2,1,0:T(8,128)(2,1)S(1)} collective-permute-done((bf16[2,2,48,768]{3,2,1,0:T(8,128)(2,1)}, bf16[2,2,48,768]{3,2,1,0:T(8,128)(2,1)S(1)}, u32[]{:S(2)}, u32[]{:S(2)}) %collective-permute-start.6) | collective-permute-done | bytes 294944 | tf_op jit(solution)/shard_map/ppermute | solution.py:722
  56.3 2.9 maximum_select_fusion
  61.4 2.1 maximum_select_fusion.5
  65.2 1.1 maximum_select_fusion.6
  66.3 1.2 maximum_select_fusion.2
  67.5 5.6 %convolution_convert_fusion.rel_ref = bf16[2432,384]{1,0:T(8,128)(2,1)} fusion(bf16[2432,768]{1,0:T(8,128)(2,1)} %pad_maximum_fusion, bf16[768,896]{1,0:T(8,128)(2,1)S(1)} %bitcast.184), kind=kOutput, calls=%fused_computation | convolution fusion | flops 1435385856 | bytes 6193152 | tf_op jit(solution)/shard_map/dot_general | solution.py:39
  73.1 5.0 %convolution_convert_fusion.1.q_ref.k_ref.v_ref = bf16[1664,768]{1,0:T(8,128)(2,1)} fusion(bf16[768,768]{1,0:T(8,128)(2,1)} %bitcast.36, bf16[384,768]{1,0:T(8,128)(2,1)S(1)} %copy-done.20, bf16[256,768]{1,0:T(8,128)(2,1)S(1)} %maximum_select_fusion.6, bf16[1024,768]{1,0:T(8,128)(2,1)S(1)} %copy-done.17), kind=kOutput, calls=%fused_computation.4 | convolution fusion | flops 1971879936 | bytes 6291456 | tf_op jit(solution)/shard_map/dot_general | solution.py:39
  78.1 17.2 %shard_map.332 = (bf16[1280,128]{1,0:T(8,128)(2,1)S(1)}, bf16[5,2,256,1408]{3,2,1,0:T(8,128)(2,1)}, f32[1280,128]{1,0:T(8,128)S(1)}) custom-call(s32[4]{0:T(128)S(1)} %bitcast.176, bf16[1664,768]{1,0:T(8,128)(2,1)} %convolution_convert_fusion.1.q_ref.k_ref.v_ref, bf16[1664,768]{1,0:T(8,128)(2,1)} %convolution_convert_fusion.1.q_ref.k_ref.v_ref, ...), custom_call_target="tpu_custom_call" | custom-call | flops 29527900160 | bytes 7208960 | tf_op jit(solution)/shard_map/pallas_call | solution.py:352
  96.1 1.4 collective-permute-start.12
  97.5 17.4 %shard_map.333 = (bf16[1280,128]{1,0:T(8,128)(2,1)S(1)}, bf16[5,2,256,1408]{3,2,1,0:T(8,128)(2,1)}, f32[1280,128]{1,0:T(8,128)S(1)}) custom-call(s32[4]{0:T(128)S(1)} %bitcast.177, bf16[1664,768]{1,0:T(8,128)(2,1)} %convolution_convert_fusion.1.q_ref.k_ref.v_ref, bf16[1664,768]{1,0:T(8,128)(2,1)} %convolution_convert_fusion.1.q_ref.k_ref.v_ref, ...), custom_call_target="tpu_custom_call" | custom-call | flops 29527900160 | bytes 7208960 | tf_op jit(solution)/shard_map/pallas_call | solution.py:352
  115.8 2.5 convolution_convert_fusion.2.q_ref.k_ref.v_ref
  118.3 17.1 %shard_map.334 = (bf16[1280,128]{1,0:T(8,128)(2,1)S(1)}, bf16[5,2,256,1408]{3,2,1,0:T(8,128)(2,1)}, f32[1280,128]{1,0:T(8,128)S(1)}) custom-call(s32[4]{0:T(128)S(1)} %bitcast.178, bf16[1664,384]{1,0:T(8,128)(2,1)} %convolution_convert_fusion.2.q_ref.k_ref.v_ref, bf16[1664,384]{1,0:T(8,128)(2,1)} %convolution_convert_fusion.2.q_ref.k_ref.v_ref, ...), custom_call_target="tpu_custom_call" | custom-call | flops 29527900160 | bytes 7208960 | tf_op jit(solution)/shard_map/pallas_call | solution.py:352
  136.9 1.5 collective-permute-start.14
  138.4 4.1 %collective-permute-done.13 = bf16[640,128]{1,0:T(8,128)(2,1)S(1)} collective-permute-done((bf16[640,128]{1,0:T(8,128)(2,1)S(1)}, bf16[640,128]{1,0:T(8,128)(2,1)S(1)}, u32[]{:S(2)}, u32[]{:S(2)}) %collective-permute-start.13) | collective-permute-done | bytes 163872 | tf_op jit(solution)/shard_map/ppermute | solution.py:713
  142.6 2.2 collective-permute-done.14
  145.3 1.1 broadcast_select_fusion.attn_ref
  146.8 1.6 collective-permute-start.24
  151.8 38.4 %shard_map.335 = (bf16[640,768]{1,0:T(8,128)(2,1)}, f32[640,768]{1,0:T(8,128)}, bf16[768,6912]{1,0:T(8,128)(2,1)}, f32[1,3072]{1,0:T(1,128)}, f32[8,768]{1,0:T(8...) custom-call(s32[1]{0:T(128)} %bitcast.side_ref, ...), custom_call_target="tpu_custom_call" | custom-call | flops 18119393280 | bytes 47185920 | tf_op jit(solution)/shard_map/pallas_call | solution.py:667
  191.6 1.6 collective-permute-start.17
  195.2 3.0 collective-permute-done.15.far_ref
  198.2 1.2 copy-done.7
  199.5 22.1 %shard_map.336 = (bf16[1664,384]{1,0:T(8,128)(2,1)S(1)}, bf16[2432,128]{1,0:T(8,128)(2,1)S(1)}, f32[8,128]{1,0:T(8,128)S(1)}) custom-call(s32[5]{0:T(128)S(1)} %pad_add_fusion.1.order_ref, bf16[1664,768]{1,0:T(8,128)(2,1)} %convolution_convert_fusion.1.q_ref.k_ref.v_ref, bf16[1664,768]{1,0:T(8,128)(2,1)} %convolution_convert_fusion.1.q_ref.k_ref.v_ref, ...), custom_call_target="tpu_custom_call" | custom-call | flops 44291850240 | bytes 7208960 | tf_op jit(solution)/shard_map/pallas_call | solution.py:384
  221.6 1.6 convolution_convert_fusion.5
  225.0 3.4 convolution_convert_fusion.9
  231.9 4.4 %all-to-all-start = ((bf16[8,56,512]{2,1,0:T(8,128)(2,1)}), bf16[8,56,512]{2,1,0:T(8,128)(2,1)S(1)}, u32[]{:S(2)}, u32[]{:S(2)}) async-start(bf16[8,56,512]{2,1,0:T(8,128)(2,1)} %add_convert_fusion.2), calls=%async_computation | async-start | bytes 917504 | tf_op jit(solution)/shard_map/all_to_all | solution.py:972
  237.4 21.4 %shard_map.337 = (bf16[1664,384]{1,0:T(8,128)(2,1)S(1)}, bf16[2432,128]{1,0:T(8,128)(2,1)S(1)}, f32[8,128]{1,0:T(8,128)S(1)}) custom-call(s32[5]{0:T(128)S(1)} %pad_add_fusion.1.order_ref, bf16[1664,768]{1,0:T(8,128)(2,1)} %convolution_convert_fusion.1.q_ref.k_ref.v_ref, bf16[1664,768]{1,0:T(8,128)(2,1)} %convolution_convert_fusion.1.q_ref.k_ref.v_ref, ...), custom_call_target="tpu_custom_call" | custom-call | flops 44291850240 | bytes 7208960 | tf_op jit(solution)/shard_map/pallas_call | solution.py:384
  259.6 4.3 %all-to-all-done = bf16[8,56,512]{2,1,0:T(8,128)(2,1)S(1)} async-done(((bf16[8,56,512]{2,1,0:T(8,128)(2,1)}), bf16[8,56,512]{2,1,0:T(8,128)(2,1)S(1)}, u32[]{:S(2)}, u32[]{:S(2)}) %all-to-all-start) | async-done | bytes 458784 | tf_op jit(solution)/shard_map/all_to_all | solution.py:972
  264.6 3.4 convolution_convert_fusion.4
  268.2 1.2 convolution_convert_fusion.8
  271.4 1.4 collective-permute-start.21
  273.8 4.1 %all-to-all-start.1 = ((bf16[8,48,512]{2,1,0:T(8,128)(2,1)}), bf16[8,48,512]{2,1,0:T(8,128)(2,1)}, u32[]{:S(2)}, u32[]{:S(2)}) async-start(bf16[8,48,512]{2,1,0:T(8,128)(2,1)} %add_convert_fusion.3), calls=%async_computation.1 | async-start | bytes 786432 | tf_op jit(solution)/shard_map/all_to_all | solution.py:972
  278.8 21.4 %shard_map.338 = (bf16[1664,384]{1,0:T(8,128)(2,1)S(1)}, bf16[2432,128]{1,0:T(8,128)(2,1)S(1)}, f32[8,128]{1,0:T(8,128)S(1)}) custom-call(s32[5]{0:T(128)S(1)} %pad_add_fusion.1.order_ref, bf16[1664,384]{1,0:T(8,128)(2,1)} %convolution_convert_fusion.2.q_ref.k_ref.v_ref, bf16[1664,384]{1,0:T(8,128)(2,1)} %convolution_convert_fusion.2.q_ref.k_ref.v_ref, ...), custom_call_target="tpu_custom_call" | custom-call | flops 44291850240 | bytes 7208960 | tf_op jit(solution)/shard_map/pallas_call | solution.py:384
  300.5 1.2 convert_reduce_fusion.3
  301.7 3.3 convolution_convert_fusion.3
  305.3 1.8 copy-done.14
  307.1 1.2 convolution_convert_fusion.7
  308.7 1.3 copy-done.30
  310.1 1.1 collective-permute-start.23
  311.2 1.1 constant_dynamic-update-slice_fusion.24
  312.3 1.1 constant_dynamic-update-slice_fusion.23
  313.4 5.3 %fusion = f32[640,768]{1,0:T(8,128)} fusion(bf16[640,1920]{1,0:T(8,128)(2,1)S(1)} %constant_dynamic-update-slice_fusion.23, bf16[768,768]{1,0:T(8,128)(2,1)} %collective-permute-done.22, bf16[768,384]{1,0:T(8,128)(2,1)} %slice.314, bf16[768,768]{1,0:T(8,128)(2,1)} %bitcast.36), kind=kOutput, calls=%fused_computation.5 | convolution fusion | flops 1896284160 | bytes 7372800 | tf_op jit(solution)/shard_map/dot_general | solution.py:43
  319.7 5.7 %all-to-all-start.2 = ((bf16[8,56,512]{2,1,0:T(8,128)(2,1)}), bf16[8,56,512]{2,1,0:T(8,128)(2,1)S(1)}, u32[]{:S(2)}, u32[]{:S(2)}) async-start(bf16[8,56,512]{2,1,0:T(8,128)(2,1)} %add_convert_fusion.1), calls=%async_computation.2 | async-start | bytes 917504 | tf_op jit(solution)/shard_map/all_to_all | solution.py:972
  325.3 3.0 add_add_fusion
  328.4 1.2 slice_bitcast_fusion
  329.6 1.2 constant_dynamic-slice_fusion.4
  330.8 1.3 collective-permute-start.26
  332.9 5.5 %all-to-all-done.2 = bf16[8,56,512]{2,1,0:T(8,128)(2,1)S(1)} async-done(((bf16[8,56,512]{2,1,0:T(8,128)(2,1)}), bf16[8,56,512]{2,1,0:T(8,128)(2,1)S(1)}, u32[]{:S(2)}, u32[]{:S(2)}) %all-to-all-start.2) | async-done | bytes 458784 | tf_op jit(solution)/shard_map/all_to_all | solution.py:972
  338.4 1.7 collective-permute-done.26
  341.6 1.1 collective-permute-start.28
  (321 shorter events, 56.2 us)
Async XLA Ops:
  7.2 141.2 %all-gather.2.cloned.1.call-start = ((), (), s32[]{:S(2)}) async-start(), calls=%async_computation.4 | async-start | bytes 11489280 | tf_op jit(solution)/shard_map/all_gather | solution.py:870
  11.6 25.1 %collective-permute-start = (bf16[48,768]{1,0:T(8,128)(2,1)S(1)}, bf16[48,768]{1,0:T(8,128)(2,1)S(1)}, u32[]{:S(2)}, u32[]{:S(2)}) collective-permute-start(bf16[48,768]{1,0:T(8,128)(2,1)S(1)} %constant_dynamic-update-slice_fusion), channel_id=1, source_target_pairs={{0,8},{1,9},{2,10},{3,11},{4,12},{5,13},{6,14},{7,15},{8,0},{9,1},... | collective-permute-start | bytes 221192 | tf_op jit(solution)/shard_map/ppermute | solution.py:722
  17.1 14.6 %copy-start.37 = (bf16[2,48]{1,0:T(2,128)(2,1)S(1)}, bf16[2,48]{1,0:T(2,128)(2,1)}, u32[]{:S(2)}) copy-start(bf16[2,48]{1,0:T(2,128)(2,1)} %param.38) | copy-start | bytes 580
  17.1 14.7 %copy-start.38 = (bf16[2,48]{1,0:T(2,128)(2,1)S(1)}, bf16[2,48]{1,0:T(2,128)(2,1)}, u32[]{:S(2)}) copy-start(bf16[2,48]{1,0:T(2,128)(2,1)} %param.39) | copy-start | bytes 580
  17.1 14.7 %slice-start.1 = ((s32[1,1408]{1,0:T(1,128)}), s32[1,1024]{1,0:T(1,128)S(1)}, s32[]{:S(2)}) async-start(s32[1,1408]{1,0:T(1,128)} %param.24), calls=%async_computation.7 | async-start | bytes 8192 | tf_op jit(solution)/shard_map/slice | solution.py:827
  17.2 19.5 %collective-permute-start.1 = (bf16[48,896]{1,0:T(8,128)(2,1)S(1)}, bf16[48,896]{1,0:T(8,128)(2,1)S(1)}, u32[]{:S(2)}, u32[]{:S(2)}) collective-permute-start(bf16[48,896]{1,0:T(8,128)(2,1)S(1)} %constant_dynamic-update-slice_fusion.6), channel_id=1, source_target_pairs={{0,2},{1,3},{2,0},{3,1},{4,6},{5,7},{6,4},{7,5},{8,10},{9,11},{10,... | collective-permute-start | bytes 258056 | tf_op jit(solution)/shard_map/ppermute | solution.py:722
  19.9 16.8 %collective-permute-start.2 = (bf16[256,768]{1,0:T(8,128)(2,1)S(1)}, bf16[256,768]{1,0:T(8,128)(2,1)S(1)}, u32[]{:S(2)}, u32[]{:S(2)}) collective-permute-start(bf16[256,768]{1,0:T(8,128)(2,1)S(1)} %get-tuple-element.158), channel_id=1, source_target_pairs={{0,16},{16,0},{1,17},{17,1},{2,18},{18,2},{3,19},{19,3},{4,20},{20... | collective-permute-start | bytes 1179656 | tf_op jit(solution)/shard_map/ppermute | solution.py:713
  21.5 19.1 %collective-permute-start.5 = (bf16[256,768]{1,0:T(8,128)(2,1)S(1)}, bf16[256,768]{1,0:T(8,128)(2,1)}, u32[]{:S(2)}, u32[]{:S(2)}) collective-permute-start(bf16[256,768]{1,0:T(8,128)(2,1)S(1)} %get-tuple-element.157), channel_id=1, source_target_pairs={{0,16},{16,0},{1,17},{17,1},{2,18},{18,2},{3,19},{19,3},{4,20},{20... | collective-permute-start | bytes 1179656 | tf_op jit(solution)/shard_map/ppermute | solution.py:713
  22.0 26.5 %collective-permute-start.8 = (bf16[192,768]{1,0:T(8,128)(2,1)}, bf16[192,768]{1,0:T(8,128)(2,1)}, u32[]{:S(2)}, u32[]{:S(2)}) collective-permute-start(bf16[192,768]{1,0:T(8,128)(2,1)} %bitcast.229), channel_id=1, source_target_pairs={{0,16},{16,0},{1,17},{17,1},{2,18},{18,2},{3,19},{19,3},{4,20},{20... | collective-permute-start | bytes 884744 | tf_op jit(solution)/shard_map/ppermute | solution.py:713
  34.3 2.3 copy-start.34
  34.3 2.3 copy-start.35
  36.6 11.0 %copy-start.31 = (bf16[48,768]{1,0:T(8,128)(2,1)S(1)}, bf16[48,768]{1,0:T(8,128)(2,1)}, u32[]{:S(2)}) copy-start(bf16[48,768]{1,0:T(8,128)(2,1)} %param.30) | copy-start | bytes 221188
  36.6 18.5 %copy-start = (s32[1,4]{1,0:T(1,128)S(1)}, s32[1,4]{1,0:T(1,128)}, u32[]{:S(2)}) copy-start(s32[1,4]{1,0:T(1,128)} %param.25) | copy-start | bytes 52
  36.7 9.4 %collective-permute-start.4 = (bf16[2,48,896]{2,1,0:T(8,128)(2,1)S(1)}, bf16[2,48,896]{2,1,0:T(8,128)(2,1)S(1)}, u32[]{:S(2)}, u32[]{:S(2)}) collective-permute-start(bf16[2,48,896]{2,1,0:T(8,128)(2,1)S(1)} %maximum_select_fusion.10), channel_id=1, source_target_pairs={{0,8},{1,9},{2,10},{3,11},{4,12},{5,13},{6,14},{7,15},{8,0},{9,1},... | collective-permute-start | bytes 516104 | tf_op jit(solution)/shard_map/ppermute | solution.py:722
  37.1 6.5 %collective-permute-start.3 = (bf16[2,48,768]{2,1,0:T(8,128)(2,1)S(1)}, bf16[2,48,768]{2,1,0:T(8,128)(2,1)S(1)}, u32[]{:S(2)}, u32[]{:S(2)}) collective-permute-start(bf16[2,48,768]{2,1,0:T(8,128)(2,1)S(1)} %maximum_select_fusion.12), channel_id=1, source_target_pairs={{0,4},{1,5},{2,6},{3,7},{4,0},{5,1},{6,2},{7,3},{8,12},{9,13},{10,... | collective-permute-start | bytes 442376 | tf_op jit(solution)/shard_map/ppermute | solution.py:722
  46.2 8.0 %collective-permute-start.7 = (bf16[2,2,48,896]{3,2,1,0:T(8,128)(2,1)S(1)}, bf16[2,2,48,896]{3,2,1,0:T(8,128)(2,1)S(1)}, u32[]{:S(2)}, u32[]{:S(2)}) collective-permute-start(bf16[2,2,48,896]{3,2,1,0:T(8,128)(2,1)S(1)} %maximum_select_fusion.7), channel_id=1, source_target_pairs={{0,4},{1,5},{2,6},{3,7},{4,0},{5,1},{6,2},{7,3},{8,12},{9,13},{10,... | collective-permute-start | bytes 1032200 | tf_op jit(solution)/shard_map/ppermute | solution.py:722
  47.0 7.1 %collective-permute-start.6 = (bf16[2,2,48,768]{3,2,1,0:T(8,128)(2,1)}, bf16[2,2,48,768]{3,2,1,0:T(8,128)(2,1)S(1)}, u32[]{:S(2)}, u32[]{:S(2)}) collective-permute-start(bf16[2,2,48,768]{3,2,1,0:T(8,128)(2,1)} %maximum_select_fusion.9), channel_id=1, source_target_pairs={{0,2},{1,3},{2,0},{3,1},{4,6},{5,7},{6,4},{7,5},{8,10},{9,11},{10,... | collective-permute-start | bytes 884744 | tf_op jit(solution)/shard_map/ppermute | solution.py:722
  48.4 7.9 %copy-start.15 = (bf16[1,512,768]{2,1,0:T(8,128)(2,1)S(1)}, bf16[1,512,768]{2,1,0:T(8,128)(2,1)}, u32[]{:S(2)}) copy-start(bf16[1,512,768]{2,1,0:T(8,128)(2,1)} %param.21) | copy-start | bytes 2359300
  54.2 275.4 %reduce-scatter.2.cloned.1.call-start = ((), (), s32[]{:S(2)}) async-start(), calls=%async_computation.5 | async-start | bytes 11280384 | tf_op jit(solution)/shard_map/reduce_scatter | solution.py:938
  54.5 9.1 %collective-permute-start.11 = (bf16[128,768]{1,0:T(8,128)(2,1)}, bf16[128,768]{1,0:T(8,128)(2,1)S(1)}, u32[]{:S(2)}, u32[]{:S(2)}) collective-permute-start(bf16[128,768]{1,0:T(8,128)(2,1)} %bitcast.15.query_ref), channel_id=1, source_target_pairs={{0,16},{16,0},{1,17},{17,1},{2,18},{18,2},{3,19},{19,3},{4,20},{20... | collective-permute-start | bytes 589832 | tf_op jit(solution)/shard_map/ppermute | solution.py:713
  59.5 4.1 %collective-permute-start.10 = (bf16[2,2,2,48,896]{4,3,2,1,0:T(8,128)(2,1)S(1)}, bf16[2,2,2,48,896]{4,3,2,1,0:T(8,128)(2,1)S(1)}, u32[]{:S(2)}, u32[]{:S(2)}) collective-permute-start(bf16[2,2,2,48,896]{4,3,2,1,0:T(8,128)(2,1)S(1)} %maximum_select_fusion.3), channel_id=1, source_target_pairs={{0,1},{1,0},{2,3},{3,2},{4,5},{5,4},{6,7},{7,6},{8,9},{9,8},{10,11... | collective-permute-start | bytes 2064392 | tf_op jit(solution)/shard_map/ppermute | solution.py:722
  59.7 3.9 %collective-permute-start.9 = (bf16[2,2,2,48,768]{4,3,2,1,0:T(8,128)(2,1)S(1)}, bf16[2,2,2,48,768]{4,3,2,1,0:T(8,128)(2,1)S(1)}, u32[]{:S(2)}, u32[]{:S(2)}) collective-permute-start(bf16[2,2,2,48,768]{4,3,2,1,0:T(8,128)(2,1)S(1)} %maximum_select_fusion.4), channel_id=1, source_target_pairs={{0,1},{1,0},{2,3},{3,2},{4,5},{5,4},{6,7},{7,6},{8,9},{9,8},{10,11... | collective-permute-start | bytes 1769480 | tf_op jit(solution)/shard_map/ppermute | solution.py:722
  66.3 48.7 %copy-start.23 = (bf16[256,768]{1,0:T(8,128)(2,1)}, bf16[256,768]{1,0:T(8,128)(2,1)S(1)}, u32[]{:S(2)}) copy-start(bf16[256,768]{1,0:T(8,128)(2,1)S(1)} %maximum_select_fusion.6) | copy-start | bytes 1179652
  67.5 5.6 %copy-start.17 = (bf16[1024,768]{1,0:T(8,128)(2,1)S(1)}, bf16[1024,768]{1,0:T(8,128)(2,1)}, u32[]{:S(2)}) copy-start(bf16[1024,768]{1,0:T(8,128)(2,1)} %maximum_select_fusion) | copy-start | bytes 4718596
  67.5 5.6 %copy-start.20 = (bf16[384,768]{1,0:T(8,128)(2,1)S(1)}, bf16[384,768]{1,0:T(8,128)(2,1)}, u32[]{:S(2)}) copy-start(bf16[384,768]{1,0:T(8,128)(2,1)} %maximum_select_fusion.5) | copy-start | bytes 1769476
  96.1 42.3 %collective-permute-start.12 = (bf16[640,128]{1,0:T(8,128)(2,1)S(1)}, bf16[640,128]{1,0:T(8,128)(2,1)S(1)}, u32[]{:S(2)}, u32[]{:S(2)}) collective-permute-start(bf16[640,128]{1,0:T(8,128)(2,1)S(1)} %pad_maximum_fusion.19), channel_id=1, source_target_pairs={{0,16},{16,0},{1,17},{17,1},{2,18},{18,2},{3,19},{19,3},{4,20},{20... | collective-permute-start | bytes 491528 | tf_op jit(solution)/shard_map/ppermute | solution.py:713
  135.4 9.8 %copy-start.8 = (f32[1280,128]{1,0:T(8,128)}, f32[1280,128]{1,0:T(8,128)S(1)}, u32[]{:S(2)}) copy-start(f32[1280,128]{1,0:T(8,128)S(1)} %get-tuple-element.125.inv_ref) | copy-start | bytes 1966084
  135.4 7.2 %collective-permute-start.13 = (bf16[640,128]{1,0:T(8,128)(2,1)S(1)}, bf16[640,128]{1,0:T(8,128)(2,1)S(1)}, u32[]{:S(2)}, u32[]{:S(2)}) collective-permute-start(bf16[640,128]{1,0:T(8,128)(2,1)S(1)} %pad_maximum_fusion.20), channel_id=1, source_target_pairs={{0,16},{16,0},{1,17},{17,1},{2,18},{18,2},{3,19},{19,3},{4,20},{20... | collective-permute-start | bytes 491528 | tf_op jit(solution)/shard_map/ppermute | solution.py:713
  136.9 7.9 %collective-permute-start.14 = (bf16[640,128]{1,0:T(8,128)(2,1)S(1)}, bf16[640,128]{1,0:T(8,128)(2,1)S(1)}, u32[]{:S(2)}, u32[]{:S(2)}) collective-permute-start(bf16[640,128]{1,0:T(8,128)(2,1)S(1)} %pad_maximum_fusion.21), channel_id=1, source_target_pairs={{0,16},{16,0},{1,17},{17,1},{2,18},{18,2},{3,19},{19,3},{4,20},{20... | collective-permute-start | bytes 491528 | tf_op jit(solution)/shard_map/ppermute | solution.py:713
  146.4 167.1 %collective-permute-start.22 = (bf16[768,768]{1,0:T(8,128)(2,1)}, bf16[768,768]{1,0:T(8,128)(2,1)}, u32[]{:S(2)}, u32[]{:S(2)}) collective-permute-start(bf16[768,768]{1,0:T(8,128)(2,1)} %bitcast.36), channel_id=1, source_target_pairs={{0,16},{16,0},{1,17},{17,1},{2,18},{18,2},{3,19},{19,3},{4,20},{20... | collective-permute-start | bytes 3538952 | tf_op jit(solution)/shard_map/ppermute | solution.py:713
  146.8 178.5 %collective-permute-start.24 = (bf16[768,384]{1,0:T(8,128)(2,1)}, bf16[768,384]{1,0:T(8,128)(2,1)}, u32[]{:S(2)}, u32[]{:S(2)}) collective-permute-start(bf16[768,384]{1,0:T(8,128)(2,1)} %slice.314), channel_id=1, source_target_pairs={{0,16},{16,0},{1,17},{17,1},{2,18},{18,2},{3,19},{19,3},{4,20},{20... | collective-permute-start | bytes 1769480 | tf_op jit(solution)/shard_map/ppermute | solution.py:713
  190.2 3.4 copy-start.19
  190.2 8.0 %copy-start.12 = (bf16[640,128]{1,0:T(8,128)(2,1)S(1)}, bf16[640,128]{1,0:T(8,128)(2,1)}, u32[]{:S(2)}) copy-start(bf16[640,128]{1,0:T(8,128)(2,1)} %get-tuple-element.101.near_ref) | copy-start | bytes 491524
  191.1 7.1 %collective-permute-start.15 = (bf16[640,128]{1,0:T(8,128)(2,1)S(1)}, bf16[640,128]{1,0:T(8,128)(2,1)S(1)}, u32[]{:S(2)}, u32[]{:S(2)}) collective-permute-start(bf16[640,128]{1,0:T(8,128)(2,1)S(1)} %copy-done.36), channel_id=1, source_target_pairs={{0,16},{16,0},{1,17},{17,1},{2,18},{18,2},{3,19},{19,3},{4,20},{20... | collective-permute-start | bytes 491528 | tf_op jit(solution)/shard_map/ppermute | solution.py:713
  191.6 44.7 %collective-permute-start.17 = (bf16[640,128]{1,0:T(8,128)(2,1)}, bf16[640,128]{1,0:T(8,128)(2,1)S(1)}, u32[]{:S(2)}, u32[]{:S(2)}) collective-permute-start(bf16[640,128]{1,0:T(8,128)(2,1)} %get-tuple-element.113), channel_id=1, source_target_pairs={{0,16},{16,0},{1,17},{17,1},{2,18},{18,2},{3,19},{19,3},{4,20},{20... | collective-permute-start | bytes 491528 | tf_op jit(solution)/shard_map/ppermute | solution.py:713
  193.1 84.7 %collective-permute-start.19 = (bf16[640,128]{1,0:T(8,128)(2,1)}, bf16[640,128]{1,0:T(8,128)(2,1)S(1)}, u32[]{:S(2)}, u32[]{:S(2)}) collective-permute-start(bf16[640,128]{1,0:T(8,128)(2,1)} %get-tuple-element.124), channel_id=1, source_target_pairs={{0,16},{16,0},{1,17},{17,1},{2,18},{18,2},{3,19},{19,3},{4,20},{20... | collective-permute-start | bytes 491528 | tf_op jit(solution)/shard_map/ppermute | solution.py:713
  199.5 22.1 %copy-start.18 = (bf16[1024,768]{1,0:T(8,128)(2,1)S(1)}, bf16[1024,768]{1,0:T(8,128)(2,1)}, u32[]{:S(2)}) copy-start(bf16[1024,768]{1,0:T(8,128)(2,1)} %maximum_select_fusion) | copy-start | bytes 4718596
  199.5 22.1 %copy-start.21 = (bf16[384,768]{1,0:T(8,128)(2,1)S(1)}, bf16[384,768]{1,0:T(8,128)(2,1)}, u32[]{:S(2)}) copy-start(bf16[384,768]{1,0:T(8,128)(2,1)} %maximum_select_fusion.5) | copy-start | bytes 1769476
  199.5 22.2 %copy-start.24 = (bf16[256,768]{1,0:T(8,128)(2,1)S(1)}, bf16[256,768]{1,0:T(8,128)(2,1)}, u32[]{:S(2)}) copy-start(bf16[256,768]{1,0:T(8,128)(2,1)} %copy-done.23) | copy-start | bytes 1179652
  221.6 2.5 copy-start.32
  221.6 2.9 copy-start.33
  225.0 3.5 copy-start.16
  228.6 2.0 collective-permute-start.16
  228.8 7.5 %copy-start.11 = (bf16[640,128]{1,0:T(8,128)(2,1)S(1)}, bf16[640,128]{1,0:T(8,128)(2,1)}, u32[]{:S(2)}) copy-start(bf16[640,128]{1,0:T(8,128)(2,1)} %get-tuple-element.112.near_ref) | copy-start | bytes 491524
  230.6 79.5 %collective-permute-start.20 = (bf16[640,384]{1,0:T(8,128)(2,1)}, bf16[640,384]{1,0:T(8,128)(2,1)}, u32[]{:S(2)}, u32[]{:S(2)}) collective-permute-start(bf16[640,384]{1,0:T(8,128)(2,1)} %pad_maximum_fusion.10), channel_id=1, source_target_pairs={{0,16},{16,0},{1,17},{17,1},{2,18},{18,2},{3,19},{19,3},{4,20},{20... | collective-permute-start | bytes 1474568 | tf_op jit(solution)/shard_map/ppermute | solution.py:713
  231.9 32.0 %all-to-all-start = ((bf16[8,56,512]{2,1,0:T(8,128)(2,1)}), bf16[8,56,512]{2,1,0:T(8,128)(2,1)S(1)}, u32[]{:S(2)}, u32[]{:S(2)}) async-start(bf16[8,56,512]{2,1,0:T(8,128)(2,1)} %add_convert_fusion.2), calls=%async_computation | async-start | bytes 917504 | tf_op jit(solution)/shard_map/all_to_all | solution.py:972
  264.6 3.5 copy-start.3
  264.6 3.5 copy-start.13
  269.5 1.9 collective-permute-start.18
  269.7 8.2 %copy-start.9 = (f32[1280,128]{1,0:T(8,128)S(1)}, f32[1280,128]{1,0:T(8,128)}, u32[]{:S(2)}) copy-start(f32[1280,128]{1,0:T(8,128)} %copy-done.8) | copy-start | bytes 1966084
  271.4 40.8 %collective-permute-start.21 = (bf16[640,384]{1,0:T(8,128)(2,1)}, bf16[640,384]{1,0:T(8,128)(2,1)}, u32[]{:S(2)}, u32[]{:S(2)}) collective-permute-start(bf16[640,384]{1,0:T(8,128)(2,1)} %pad_maximum_fusion.11), channel_id=1, source_target_pairs={{0,16},{16,0},{1,17},{17,1},{2,18},{18,2},{3,19},{19,3},{4,20},{20... | collective-permute-start | bytes 1474568 | tf_op jit(solution)/shard_map/ppermute | solution.py:713
  273.8 26.7 %all-to-all-start.1 = ((bf16[8,48,512]{2,1,0:T(8,128)(2,1)}), bf16[8,48,512]{2,1,0:T(8,128)(2,1)}, u32[]{:S(2)}, u32[]{:S(2)}) async-start(bf16[8,48,512]{2,1,0:T(8,128)(2,1)} %add_convert_fusion.3), calls=%async_computation.1 | async-start | bytes 786432 | tf_op jit(solution)/shard_map/all_to_all | solution.py:972
  301.7 39.6 %copy-start.25 = (f32[48,512]{1,0:T(8,128)}, f32[48,512]{1,0:T(8,128)S(1)}, u32[]{:S(2)}) copy-start(f32[48,512]{1,0:T(8,128)S(1)} %convert_reduce_fusion.3) | copy-start | bytes 294916
  305.0 2.1 copy-start.14
  308.3 1.7 copy-start.30
  308.4 10.4 %collective-permute-start.25 = (bf16[8,56,512]{2,1,0:T(8,128)(2,1)S(1)}, bf16[8,56,512]{2,1,0:T(8,128)(2,1)S(1)}, u32[]{:S(2)}, u32[]{:S(2)}) collective-permute-start(bf16[8,56,512]{2,1,0:T(8,128)(2,1)S(1)} %pad_maximum_fusion.14), channel_id=1, source_target_pairs={{0,1},{1,0},{2,3},{3,2},{4,5},{5,4},{6,7},{7,6},{8,9},{9,8},{10,11... | collective-permute-start | bytes 1376264 | tf_op jit(solution)/shard_map/ppermute | solution.py:722
  310.1 15.2 %collective-permute-start.23 = (bf16[640,384]{1,0:T(8,128)(2,1)S(1)}, bf16[640,384]{1,0:T(8,128)(2,1)S(1)}, u32[]{:S(2)}, u32[]{:S(2)}) collective-permute-start(bf16[640,384]{1,0:T(8,128)(2,1)S(1)} %pad_maximum_fusion.12), channel_id=1, source_target_pairs={{0,16},{16,0},{1,17},{17,1},{2,18},{18,2},{3,19},{19,3},{4,20},{20... | collective-permute-start | bytes 1474568 | tf_op jit(solution)/shard_map/ppermute | solution.py:713
  319.7 18.7 %all-to-all-start.2 = ((bf16[8,56,512]{2,1,0:T(8,128)(2,1)}), bf16[8,56,512]{2,1,0:T(8,128)(2,1)S(1)}, u32[]{:S(2)}, u32[]{:S(2)}) async-start(bf16[8,56,512]{2,1,0:T(8,128)(2,1)} %add_convert_fusion.1), calls=%async_computation.2 | async-start | bytes 917504 | tf_op jit(solution)/shard_map/all_to_all | solution.py:972
  329.6 11.6 %copy-start.22 = (f32[56,512]{1,0:T(8,128)S(1)}, f32[56,512]{1,0:T(8,128)}, u32[]{:S(2)}) copy-start(f32[56,512]{1,0:T(8,128)} %convert_reduce_fusion.2) | copy-start | bytes 344068
  330.8 9.4 %collective-permute-start.26 = (bf16[1,24,6912]{2,1,0:T(8,128)(2,1)S(1)}, bf16[1,24,6912]{2,1,0:T(8,128)(2,1)}, u32[]{:S(2)}, u32[]{:S(2)}) collective-permute-start(bf16[1,24,6912]{2,1,0:T(8,128)(2,1)S(1)} %get-tuple-element.162), channel_id=1, source_target_pairs={{0,16},{16,0},{1,17},{17,1},{2,18},{18,2},{3,19},{19,3},{4,20},{20... | collective-permute-start | bytes 995336 | tf_op jit(solution)/shard_map/ppermute | solution.py:713
  341.2 3.3 copy-start.27
  341.4 3.5 slice-start
  341.6 7.5 %collective-permute-start.28 = (bf16[512]{0:T(512)(128)(2,1)S(1)}, bf16[512]{0:T(512)(128)(2,1)S(1)}, u32[]{:S(2)}, u32[]{:S(2)}) collective-permute-start(bf16[512]{0:T(512)(128)(2,1)S(1)} %fusion.35), channel_id=1, source_target_pairs={{0,16},{16,0},{1,17},{17,1},{2,18},{18,2},{3,19},{19,3},{4,20},{20... | collective-permute-start | bytes 3080 | tf_op jit(solution)/shard_map/ppermute | solution.py:713
  342.7 8.7 %collective-permute-start.27 = (bf16[24,1152]{1,0:T(8,128)(2,1)S(1)}, bf16[24,1152]{1,0:T(8,128)(2,1)S(1)}, u32[]{:S(2)}, u32[]{:S(2)}) collective-permute-start(bf16[24,1152]{1,0:T(8,128)(2,1)S(1)} %dynamic-slice_convert_fusion), channel_id=1, source_target_pairs={{0,16},{16,0},{1,17},{17,1},{2,18},{18,2},{3,19},{19,3},{4,20},{20... | collective-permute-start | bytes 165896 | tf_op jit(solution)/shard_map/ppermute | solution.py:713
  (11 other events, 10.9 us)
Sparse Core Ops, SparseCore 0:
  54.3 88.3 all-gather.1
  190.4 135.9 reduce-scatter.1
